TPU v7x, 512 devices: a whole 4x4x16 slice. The times are simulated.
512 devices in a mesh: seq: 32 (over z, core), head: 16 (over y, x).
Axes of the slice: x: 4, y: 4, z: 16, core: 2. Of those that a mesh axis runs over, the one named last changes fastest.
Arguments:
- queries: bfloat16 [65536, 2048], P('seq', 'head'), may hold values from -64 to 64
- keys: bfloat16 [65536, 2048], P('seq', 'head'), may hold values from -24 to 24
- values: bfloat16 [65536, 2048], P('seq', 'head'), may hold values from -6 to 6
- d_out: bfloat16 [65536, 2048], P('seq', 'head'), may hold values from -6 to 6
- cluster_id: int32 [65536, 1], P('seq'), may hold values from 0 to 255; in each aligned block of 2048 rows (0 to 2047, 2048 to 4095, ...) at most 12 rows name the same one
Outputs:
- attn_out: bfloat16 [65536, 2048], P('seq', 'head')
- d_queries: bfloat16 [65536, 2048], P('seq', 'head')
- d_keys: bfloat16 [65536, 2048], P('seq', 'head')
- d_values: bfloat16 [65536, 2048], P('seq', 'head')
- centroids: float32 [256, 2048], P(None, 'head')
Inputs may be any that keep to these rules, and one draw needn't show every extreme that they name: `cluster_id`: among the 2048 tokens of one device no cluster appears more than 12 times, and in every draw some cluster appears exactly 12 times among the tokens of some device; every cluster has at least one token.
All inputs are finite; a program needn't handle non-finite values.
Results may differ from a plain program's by a relative error of at most 0.0051.
Values may be sent and summed in bfloat16 or wider, within the bound.
No kernel may reach another device: no remote copies, remote signals or barrier semaphores. Data moves between devices by JAX's collectives and lax.ppermute only.
A program may use at most 64 MiB of HBM per device.

v0:
```python
import jax
import jax.numpy as jnp
from jax import lax
from jax.sharding import PartitionSpec as P

DH = 128
CLUSTERS = 256
CAPC = 12
D = 2048


EPSILON = 1e-06
NEGATIVE = -1e30


def weights_part(query_rows, key_rows, visible, heads_here):
    slot_count = query_rows.shape[0]
    query_heads = query_rows.reshape(slot_count, heads_here, -1)
    key_heads = key_rows.reshape(slot_count, heads_here, -1)
    scaling = query_heads.shape[2] ** (-0.5)
    scores = (
        jnp.einsum("shd,thd->hst", query_heads, key_heads, preferred_element_type=jnp.float32)
        * scaling
    )
    scores = jnp.where(visible[None], scores, NEGATIVE)
    row_top = jnp.max(scores, axis=2, keepdims=True)
    weights = jnp.exp(scores - row_top)
    attention = weights / jnp.sum(weights, axis=2, keepdims=True)
    return (attention, attention.astype(jnp.bfloat16))


def output_part(attention_b, value_rows, heads_here):
    slot_count = value_rows.shape[0]
    value_heads = value_rows.reshape(slot_count, heads_here, -1)
    attended = jnp.einsum(
        "hst,thd->shd", attention_b, value_heads, preferred_element_type=jnp.float32
    )
    return attended.astype(jnp.bfloat16).reshape(slot_count, -1)


def backward_part(query_rows, key_rows, value_rows, grad_rows, attention, attention_b, heads_here):
    slot_count = query_rows.shape[0]
    query_heads = query_rows.reshape(slot_count, heads_here, -1)
    key_heads = key_rows.reshape(slot_count, heads_here, -1)
    value_heads = value_rows.reshape(slot_count, heads_here, -1)
    grad_heads = grad_rows.reshape(slot_count, heads_here, -1)
    scaling = query_heads.shape[2] ** (-0.5)
    grad_weights = jnp.einsum(
        "shd,thd->hst", grad_heads, value_heads, preferred_element_type=jnp.float32
    )
    row_delta = jnp.sum(attention * grad_weights, axis=2, keepdims=True)
    grad_scores = (attention * (grad_weights - row_delta)).astype(jnp.bfloat16)
    grad_query = (
        jnp.einsum("hst,thd->shd", grad_scores, key_heads, preferred_element_type=jnp.float32)
        * scaling
    )
    grad_key = (
        jnp.einsum("hst,shd->thd", grad_scores, query_heads, preferred_element_type=jnp.float32)
        * scaling
    )
    grad_value = jnp.einsum(
        "hst,shd->thd", attention_b, grad_heads, preferred_element_type=jnp.float32
    )
    return (
        grad_query.astype(jnp.bfloat16).reshape(slot_count, -1),
        grad_key.astype(jnp.bfloat16).reshape(slot_count, -1),
        grad_value.astype(jnp.bfloat16).reshape(slot_count, -1),
    )


def body(queries, keys, values, d_out, cluster_id):
    tokens_here, feature_width = queries.shape
    heads_here = feature_width // DH
    seq_count = lax.axis_size("seq")
    slot_count = seq_count * CAPC
    cluster_row = cluster_id[:, 0]
    member = (cluster_row[:, None] == jnp.arange(CLUSTERS, dtype=jnp.int32)[None, :]).astype(
        jnp.int32
    )
    ordinal = jnp.sum((jnp.cumsum(member, axis=0) - 1) * member, axis=1)
    local_counts = jnp.sum(member, axis=0)
    slot_flat = cluster_row * CAPC + ordinal

    def pack_rows(rows):
        buffer = jnp.zeros((CLUSTERS * CAPC, feature_width), rows.dtype).at[slot_flat].set(rows)
        return buffer.reshape(CLUSTERS, CAPC, feature_width)

    def unpack_rows(block):
        return block.reshape(CLUSTERS * CAPC, feature_width)[slot_flat]

    count_column = local_counts.astype(jnp.float32).reshape(CLUSTERS, 1).astype(jnp.bfloat16)
    positions = jnp.arange(slot_count, dtype=jnp.int32)
    row_index = positions[:, None]
    column_index = positions[None, :]

    def visible_of(filled):
        return filled[None, :] & (column_index <= row_index) | (column_index == row_index)

    query_in, key_in, value_in, count_in = (
        lax.all_to_all(pack_rows(queries), "seq", split_axis=0, concat_axis=1, tiled=True),
        lax.all_to_all(pack_rows(keys), "seq", split_axis=0, concat_axis=1, tiled=True),
        lax.all_to_all(pack_rows(values), "seq", split_axis=0, concat_axis=1, tiled=True),
        lax.all_to_all(count_column, "seq", split_axis=0, concat_axis=1, tiled=True),
    )
    counts = jnp.repeat(count_in.astype(jnp.int32), CAPC, axis=1)
    filled = (positions % CAPC)[None, :] < counts

    def forward_only(inputs):
        query_rows, key_rows, value_rows, fill_row = inputs
        attention, attention_b = weights_part(
            query_rows, key_rows, visible_of(fill_row), heads_here
        )
        return (output_part(attention_b, value_rows, heads_here), attention, attention_b)

    attended_all, attention_all, attention_b_all = lax.map(
        forward_only, (query_in, key_in, value_in, filled)
    )
    attn_back = lax.all_to_all(attended_all, "seq", split_axis=1, concat_axis=0, tiled=True)
    grad_in = lax.all_to_all(pack_rows(d_out), "seq", split_axis=0, concat_axis=1, tiled=True)

    def backward_only(inputs):
        query_rows, key_rows, value_rows, grad_rows, attention, attention_b = inputs
        return backward_part(
            query_rows, key_rows, value_rows, grad_rows, attention, attention_b, heads_here
        )

    grad_query_all, grad_key_all, grad_value_all = lax.map(
        backward_only, (query_in, key_in, value_in, grad_in, attention_all, attention_b_all)
    )
    query_back, key_back, value_back = (
        lax.all_to_all(grad_query_all, "seq", split_axis=1, concat_axis=0, tiled=True),
        lax.all_to_all(grad_key_all, "seq", split_axis=1, concat_axis=0, tiled=True),
        lax.all_to_all(grad_value_all, "seq", split_axis=1, concat_axis=0, tiled=True),
    )
    key_float = keys.astype(jnp.float32)
    norm_total = lax.psum(jnp.sum(key_float * key_float, axis=1), "head")
    unit_keys = key_float / jnp.sqrt(norm_total / D + EPSILON)[:, None]
    partial_sums = jnp.dot(member.astype(jnp.float32).T, unit_keys, precision=lax.Precision.HIGHEST)
    total_sums, counts = lax.psum((partial_sums, local_counts.astype(jnp.float32)), "seq")
    cluster_means = total_sums / counts[:, None]
    spread = lax.psum(jnp.sum(cluster_means * cluster_means, axis=1), "head")
    centroids = cluster_means / jnp.sqrt(spread / D + EPSILON)[:, None]
    return (
        unpack_rows(attn_back),
        unpack_rows(query_back),
        unpack_rows(key_back),
        unpack_rows(value_back),
        centroids,
    )


def solution(mesh):
    in_specs = (
        P("seq", "head"),
        P("seq", "head"),
        P("seq", "head"),
        P("seq", "head"),
        P("seq", None),
    )
    out_specs = (
        P("seq", "head"),
        P("seq", "head"),
        P("seq", "head"),
        P("seq", "head"),
        P(None, "head"),
    )
    return jax.shard_map(body, mesh=mesh, in_specs=in_specs, out_specs=out_specs, check_vma=False)
```

profile of v0, /device:TPU:32, one launch (start us, length us, event | category | flops | bytes accessed | tf_op | source)
XLA Modules:
  0.0 808.7 jit_solution(6762640595089615802)
XLA Ops:
  11.6 15.4 %all-to-all-start.1 = ((bf16[32,8,1]{1,2,0:T(2,128)(2,1)}), bf16[32,8,1]{1,2,0:T(2,128)(2,1)S(1)}, u32[]{:S(2)}, u32[]{:S(2)}) async-start(bf16[32,8,1]{1,2,0:T(2,128)(2,1)} %convert_element_type.114), calls=%async_computation.1 | async-start | bytes 32768 | tf_op jit(solution)/shard_map/all_to_all | solution.py:103
  27.0 6.3 scatter_custom_fusion
  38.1 8.6 %all-to-all-start = ((bf16[256,12,128]{2,1,0:T(8,128)(2,1)}), bf16[256,12,128]{2,1,0:T(8,128)(2,1)S(1)}, u32[]{:S(2)}, u32[]{:S(2)}) async-start(bf16[256,12,128]{2,1,0:T(8,128)(2,1)} %reshape.201), calls=%async_computation | async-start | bytes 2097152 | tf_op jit(solution)/shard_map/all_to_all | solution.py:102
  54.2 46.6 %all-to-all-done = bf16[256,12,128]{2,1,0:T(8,128)(2,1)S(1)} async-done(((bf16[256,12,128]{2,1,0:T(8,128)(2,1)}), bf16[256,12,128]{2,1,0:T(8,128)(2,1)S(1)}, u32[]{:S(2)}, u32[]{:S(2)}) %all-to-all-start) | async-done | bytes 786464 | tf_op jit(solution)/shard_map/all_to_all | solution.py:102
  114.1 46.6 %all-to-all-done.2 = bf16[256,12,128]{2,1,0:T(8,128)(2,1)S(1)} async-done(((bf16[256,12,128]{2,1,0:T(8,128)(2,1)}), bf16[256,12,128]{2,1,0:T(8,128)(2,1)S(1)}, u32[]{:S(2)}, u32[]{:S(2)}) %all-to-all-start.2) | async-done | bytes 786464 | tf_op jit(solution)/shard_map/all_to_all | solution.py:100
  160.6 6.3 all-to-all-start.3
  167.0 7.1 scatter_custom_fusion.3
  178.1 42.9 %all-to-all-done.3 = bf16[256,12,128]{2,1,0:T(8,128)(2,1)S(1)} async-done(((bf16[256,12,128]{2,1,0:T(8,128)(2,1)}), bf16[256,12,128]{2,1,0:T(8,128)(2,1)S(1)}, u32[]{:S(2)}, u32[]{:S(2)}) %all-to-all-start.3) | async-done | bytes 786464 | tf_op jit(solution)/shard_map/all_to_all | solution.py:101
  221.1 6.3 all-to-all-start.5
  228.8 33.9 %while.31 = (s32[]{:T(128)}, bf16[8,384,128]{1,2,0:T(8,128)(2,1)S(1)}, f32[8,1,384,384]{2,3,1,0:T(8,128)}, bf16[8,1,384,384]{2,3,1,0:T(8,128)(2,1)}, bf16[8,384,...) while((s32[]{:T(128)}, ...), condition=%wide.region_10.11_spmd.clone.clone, body=%wide.region_7.10_spmd.clone.clone.sunk | while | flops 78052608 | bytes 4246369 | solution.py:115
  262.7 18.8 %all-to-all-done.5 = bf16[256,12,128]{2,1,0:T(8,128)(2,1)S(1)} async-done(((bf16[256,12,128]{2,1,0:T(8,128)(2,1)}), bf16[256,12,128]{2,1,0:T(8,128)(2,1)S(1)}, u32[]{:S(2)}, u32[]{:S(2)}) %all-to-all-start.5) | async-done | bytes 786464 | tf_op jit(solution)/shard_map/all_to_all | solution.py:119
  282.1 49.0 %while.30 = (s32[]{:T(128)}, bf16[8,384,128]{1,2,0:T(8,128)(2,1)S(1)}, bf16[8,384,128]{1,2,0:T(8,128)(2,1)S(1)}, bf16[8,384,128]{1,2,0:T(8,128)(2,1)S(1)}, bf16[...) while((s32[]{:T(128)}, ...), condition=%wide.region_14.15_spmd, body=%wide.region_12.14_spmd.sunk | while | flops 151977600 | bytes 4333681 | solution.py:127
  332.5 6.3 all-to-all-start.8
  340.1 42.2 %all-to-all-done.8 = bf16[8,384,128]{2,0,1:T(8,128)(2,1)S(1)} async-done(((bf16[8,384,128]{2,0,1:T(8,128)(2,1)}), bf16[8,384,128]{2,0,1:T(8,128)(2,1)S(1)}, u32[]{:S(2)}, u32[]{:S(2)}) %all-to-all-start.8) | async-done | bytes 786464 | tf_op jit(solution)/shard_map/all_to_all | solution.py:133
  389.4 42.2 %all-to-all-done.7 = bf16[8,384,128]{2,0,1:T(8,128)(2,1)S(1)} async-done(((bf16[8,384,128]{2,0,1:T(8,128)(2,1)}), bf16[8,384,128]{2,0,1:T(8,128)(2,1)S(1)}, u32[]{:S(2)}, u32[]{:S(2)}) %all-to-all-start.7) | async-done | bytes 786464 | tf_op jit(solution)/shard_map/all_to_all | solution.py:132
  438.5 42.2 %all-to-all-done.6 = bf16[8,384,128]{2,0,1:T(8,128)(2,1)S(1)} async-done(((bf16[8,384,128]{2,0,1:T(8,128)(2,1)}), bf16[8,384,128]{2,0,1:T(8,128)(2,1)S(1)}, u32[]{:S(2)}, u32[]{:S(2)}) %all-to-all-start.6) | async-done | bytes 786464 | tf_op jit(solution)/shard_map/all_to_all | solution.py:131
  488.4 41.2 %psum.28 = f32[2048]{0:T(1024)S(1)} all-reduce(f32[2048]{0:T(1024)S(1)} %fusion.52), channel_id=1, replica_groups=mesh['seq'=32,'head'=16] {'head'}, use_global_device_ids=true, to_apply=%region_16.17 | all-reduce | flops 2048 | bytes 16384 | tf_op jit(solution)/shard_map/psum | solution.py:136
  533.6 42.8 %psum.30 = f32[256]{0:T(256)S(1)} all-reduce(f32[256]{0:T(256)S(1)} %get-tuple-element.259), channel_id=1, replica_groups=mesh['seq'=32,'head'=16] {'seq'}, use_global_device_ids=true, to_apply=%region_18.19 | all-reduce | flops 256 | bytes 2048 | tf_op jit(solution)/shard_map/psum | solution.py:139
  576.4 147.0 %all-reduce.2.cloned.1.call-done = f32[256,128]{1,0:T(8,128)} async-done(((f32[256,128]{1,0:T(8,128)}), f32[256,128]{1,0:T(8,128)}) %all-reduce.2.cloned.1.call-update) | async-done | bytes 131088 | tf_op jit(solution)/shard_map/psum | solution.py:139
  724.5 40.5 %psum.31 = f32[256]{0:T(256)S(1)} all-reduce(f32[256]{0:T(256)S(1)} %multiply_reduce_fusion), channel_id=1, replica_groups=mesh['seq'=32,'head'=16] {'head'}, use_global_device_ids=true, to_apply=%region_20.21 | all-reduce | flops 256 | bytes 2048 | tf_op jit(solution)/shard_map/psum | solution.py:141
  767.6 8.1 gather_fusion.3
  775.6 8.0 gather_fusion.2
  784.1 8.1 gather_fusion.1
  793.8 8.1 gather_fusion
  (166 shorter events, 152.2 us)
Async XLA Ops:
  8.6 1.2 copy-start.6
  11.6 26.5 %all-to-all-start.1 = ((bf16[32,8,1]{1,2,0:T(2,128)(2,1)}), bf16[32,8,1]{1,2,0:T(2,128)(2,1)S(1)}, u32[]{:S(2)}, u32[]{:S(2)}) async-start(bf16[32,8,1]{1,2,0:T(2,128)(2,1)} %convert_element_type.114), calls=%async_computation.1 | async-start | bytes 32768 | tf_op jit(solution)/shard_map/all_to_all | solution.py:103
  38.1 62.7 %all-to-all-start = ((bf16[256,12,128]{2,1,0:T(8,128)(2,1)}), bf16[256,12,128]{2,1,0:T(8,128)(2,1)S(1)}, u32[]{:S(2)}, u32[]{:S(2)}) async-start(bf16[256,12,128]{2,1,0:T(8,128)(2,1)} %reshape.201), calls=%async_computation | async-start | bytes 2097152 | tf_op jit(solution)/shard_map/all_to_all | solution.py:102
  100.8 59.8 %all-to-all-start.2 = ((bf16[256,12,128]{2,1,0:T(8,128)(2,1)}), bf16[256,12,128]{2,1,0:T(8,128)(2,1)S(1)}, u32[]{:S(2)}, u32[]{:S(2)}) async-start(bf16[256,12,128]{2,1,0:T(8,128)(2,1)} %reshape.203), calls=%async_computation.2 | async-start | bytes 2097152 | tf_op jit(solution)/shard_map/all_to_all | solution.py:100
  160.6 60.4 %all-to-all-start.3 = ((bf16[256,12,128]{2,1,0:T(8,128)(2,1)}), bf16[256,12,128]{2,1,0:T(8,128)(2,1)S(1)}, u32[]{:S(2)}, u32[]{:S(2)}) async-start(bf16[256,12,128]{2,1,0:T(8,128)(2,1)} %reshape.204), calls=%async_computation.3 | async-start | bytes 2097152 | tf_op jit(solution)/shard_map/all_to_all | solution.py:101
  221.1 60.4 %all-to-all-start.5 = ((bf16[256,12,128]{2,1,0:T(8,128)(2,1)}), bf16[256,12,128]{2,1,0:T(8,128)(2,1)S(1)}, u32[]{:S(2)}, u32[]{:S(2)}) async-start(bf16[256,12,128]{2,1,0:T(8,128)(2,1)} %reshape.206), calls=%async_computation.5 | async-start | bytes 2097152 | tf_op jit(solution)/shard_map/all_to_all | solution.py:119
  262.7 19.0 %copy-start.4 = (bf16[8,384,128]{2,1,0:T(8,128)(2,1)}, bf16[8,384,128]{2,1,0:T(8,128)(2,1)S(1)}, u32[]{:S(2)}) copy-start(bf16[8,384,128]{2,1,0:T(8,128)(2,1)S(1)} %get-tuple-element.450) | copy-start | bytes 2359300
  262.7 19.1 %copy-start.2 = (bf16[8,384,128]{1,2,0:T(8,128)(2,1)}, bf16[8,384,128]{1,2,0:T(8,128)(2,1)S(1)}, u32[]{:S(2)}) copy-start(bf16[8,384,128]{1,2,0:T(8,128)(2,1)S(1)} %get-tuple-element.119) | copy-start | bytes 2359300
  332.5 49.9 %all-to-all-start.8 = ((bf16[8,384,128]{2,0,1:T(8,128)(2,1)}), bf16[8,384,128]{2,0,1:T(8,128)(2,1)S(1)}, u32[]{:S(2)}, u32[]{:S(2)}) async-start(bf16[8,384,128]{2,0,1:T(8,128)(2,1)} %copy.69), calls=%async_computation.8 | async-start | bytes 1572864 | tf_op jit(solution)/shard_map/all_to_all | solution.py:133
  340.1 97.0 %copy-start.3 = (bf16[8,384,128]{1,2,0:T(8,128)(2,1)S(1)}, bf16[8,384,128]{1,2,0:T(8,128)(2,1)}, u32[]{:S(2)}) copy-start(bf16[8,384,128]{1,2,0:T(8,128)(2,1)} %copy-done.2) | copy-start | bytes 2359300
  382.3 49.2 %all-to-all-start.7 = ((bf16[8,384,128]{2,0,1:T(8,128)(2,1)}), bf16[8,384,128]{2,0,1:T(8,128)(2,1)S(1)}, u32[]{:S(2)}, u32[]{:S(2)}) async-start(bf16[8,384,128]{2,0,1:T(8,128)(2,1)} %copy.67), calls=%async_computation.7 | async-start | bytes 1572864 | tf_op jit(solution)/shard_map/all_to_all | solution.py:132
  431.5 49.2 %all-to-all-start.6 = ((bf16[8,384,128]{2,0,1:T(8,128)(2,1)}), bf16[8,384,128]{2,0,1:T(8,128)(2,1)S(1)}, u32[]{:S(2)}, u32[]{:S(2)}) async-start(bf16[8,384,128]{2,0,1:T(8,128)(2,1)} %copy.65), calls=%async_computation.6 | async-start | bytes 1572864 | tf_op jit(solution)/shard_map/all_to_all | solution.py:131
  438.5 91.1 %copy-start.5 = (bf16[2048,128]{1,0:T(8,128)(2,1)S(1)}, bf16[2048,128]{1,0:T(8,128)(2,1)}, u32[]{:S(2)}) copy-start(bf16[2048,128]{1,0:T(8,128)(2,1)} %param.10) | copy-start | bytes 1572868
  480.7 52.9 %copy-start = (bf16[8,384,128]{2,0,1:T(8,128)(2,1)}, bf16[8,384,128]{2,0,1:T(8,128)(2,1)S(1)}, u32[]{:S(2)}) copy-start(bf16[8,384,128]{2,0,1:T(8,128)(2,1)S(1)} %all-to-all-done.6) | copy-start | bytes 2359300
  480.7 311.5 %all-to-all-start.4 = ((bf16[8,384,128]{2,0,1:T(8,128)(2,1)}), bf16[8,384,128]{2,0,1:T(8,128)(2,1)}, u32[]{:S(2)}, u32[]{:S(2)}) async-start(bf16[8,384,128]{2,0,1:T(8,128)(2,1)} %copy.56), calls=%async_computation.4 | async-start | bytes 1572864 | tf_op jit(solution)/shard_map/all_to_all | solution.py:118
  487.0 236.4 %all-reduce.2.cloned.1.call-start = ((), (), s32[]{:S(2)}) async-start(), calls=%async_computation.9 | async-start | bytes 262144 | tf_op jit(solution)/shard_map/psum | solution.py:139
  775.6 8.0 copy-start.1
Sparse Core Ops, SparseCore 0:
  533.7 189.6 all-reduce.1
where the time goes:
time: 812 us; the launch traced here: 809 us
  waiting for transfers between devices  432 us (53%)
  blocking collectives  125 us (15%)
  local copies, waits for them, and re-layouts  78.9 us (10%)
  starting transfers between devices  66.3 us (8%)
  matrix products  62.2 us (8%)
  other arithmetic  29.8 us (4%)
  between operations  14.5 us (2%)
    psum x1, waiting for transfers between devices, body(): lax.psum((partial_sums, local_counts.astype(jnp.float32)), 'seq')  147 us
    all_to_all x1, waiting for transfers between devices, body(): lax.all_to_all(pack_rows(values), 'seq', split_axis=0, concat_axis=1, til...  46.6 us
    all_to_all x1, waiting for transfers between devices, body(): lax.all_to_all(pack_rows(queries), 'seq', split_axis=0, concat_axis=1, ti...  46.6 us
    all_to_all x1, waiting for transfers between devices, body(): lax.all_to_all(pack_rows(keys), 'seq', split_axis=0, concat_axis=1, tiled...  42.9 us
    psum x1, blocking collectives, body(): lax.psum((partial_sums, local_counts.astype(jnp.float32)), 'seq')  42.8 us
    all_to_all x1, waiting for transfers between devices, body(): lax.all_to_all(grad_value_all, 'seq', split_axis=1, concat_axis=0, tiled=...  42.2 us
    all_to_all x1, waiting for transfers between devices, body(): lax.all_to_all(grad_query_all, 'seq', split_axis=1, concat_axis=0, tiled=...  42.2 us
    all_to_all x1, waiting for transfers between devices, body(): lax.all_to_all(grad_key_all, 'seq', split_axis=1, concat_axis=0, tiled=True)  42.2 us
  transfers between devices with their start and end apart: 10, of which 9 were waited for; matrix products, arithmetic and copies ran while one was open for 13% of the time, Pallas kernels for 0%

commit v1 on v0

v1 whole, which is shorter than its diff:
```python
import functools

import jax
import jax.numpy as jnp
from jax import lax
from jax.experimental import pallas as pl
from jax.experimental.pallas import tpu as pltpu
from jax.sharding import PartitionSpec as P

DH = 128
CLUSTERS = 256
CAPC = 12
D = 2048
N_SEQ = 32
OWN = CLUSTERS // N_SEQ
SLOTS = N_SEQ * CAPC
GROUP = 4
GROUPS = N_SEQ // GROUP
PIECE = GROUP * CAPC
ROWS_SHORT = 80
ROWS_FULL = OWN * CAPC
EPSILON = 1e-06
NEGATIVE = -1e30
VMEM = 56 * 1024 * 1024


def iota(shape, dim):
    return lax.broadcasted_iota(jnp.int32, shape, dim)


def one_hot(mask):
    return jnp.where(mask, 1.0, 0.0).astype(jnp.bfloat16)


def dot(a, b, ca, cb):
    return lax.dot_general(a, b, (((ca,), (cb,)), ((), ())), preferred_element_type=jnp.float32)


def pack_kernel(place_ref, q_ref, k_ref, v_ref, g_ref, out_ref, all_ref):
    step = pl.program_id(0)

    @pl.when(step == 0)
    def _():
        for i, ref in enumerate((q_ref, k_ref, v_ref, g_ref)):
            all_ref[:, i * DH : (i + 1) * DH] = ref[...]

    rows = out_ref.shape[0]
    wanted = iota((rows, place_ref.shape[1]), 0) + step * rows
    out_ref[...] = dot(one_hot(wanted == place_ref[...]), all_ref[...], 1, 0).astype(jnp.bfloat16)


def pack(place_row, arrays, rows):
    tokens = place_row.shape[1]
    whole = pl.BlockSpec((tokens, DH), lambda i: (0, 0))
    return pl.pallas_call(
        pack_kernel,
        grid=(GROUPS,),
        in_specs=[pl.BlockSpec((1, tokens), lambda i: (0, 0))] + [whole] * 4,
        out_specs=pl.BlockSpec((GROUP * rows, 4 * DH), lambda i: (i, 0)),
        out_shape=jax.ShapeDtypeStruct((N_SEQ * rows, 4 * DH), jnp.bfloat16),
        scratch_shapes=[pltpu.VMEM((tokens, 4 * DH), jnp.bfloat16)],
        compiler_params=pltpu.CompilerParams(vmem_limit_bytes=VMEM),
        name="pack",
    )(place_row, *arrays)


def unpack_kernel(place_ref, in_ref, *out_refs):
    tokens = place_ref.shape[0]
    chosen = one_hot(place_ref[...] == iota((tokens, in_ref.shape[0]), 1))
    rows = dot(chosen, in_ref[...], 1, 0).astype(jnp.bfloat16)
    for i, ref in enumerate(out_refs):
        ref[...] = rows[:, i * DH : (i + 1) * DH]


def unpack(place_column, block):
    tokens = place_column.shape[0]
    tile = 256
    return pl.pallas_call(
        unpack_kernel,
        grid=(tokens // tile,),
        in_specs=[
            pl.BlockSpec((tile, 1), lambda i: (i, 0)),
            pl.BlockSpec(block.shape, lambda i: (0, 0)),
        ],
        out_specs=[pl.BlockSpec((tile, DH), lambda i: (i, 0))] * 4,
        out_shape=[jax.ShapeDtypeStruct((tokens, DH), jnp.bfloat16)] * 4,
        compiler_params=pltpu.CompilerParams(vmem_limit_bytes=VMEM),
        name="unpack",
    )(place_column, block)


def attention_kernel(
    rows, place_ref, fill_ref, in_ref, out_ref, key_ref, square_ref, x_ref, y_ref, p_ref, s_ref
):
    part = GROUP * rows
    scaling = DH**-0.5

    def chosen(g):
        return one_hot(iota((part, OWN * PIECE), 0) == place_ref[pl.ds(g, 1), :])

    def spread(g, _):
        block = in_ref[pl.ds(pl.multiple_of(g * part, part), part), :]
        full = dot(chosen(g), block, 0, 0).astype(jnp.bfloat16)
        for k in range(OWN):
            at = pl.multiple_of(k * SLOTS + g * PIECE, 16)
            x_ref[pl.ds(at, PIECE), :] = full[k * PIECE : (k + 1) * PIECE]
        return 0

    lax.fori_loop(0, GROUPS, spread, 0)
    p_ref[...] = jnp.zeros_like(p_ref)
    s_ref[...] = jnp.zeros_like(s_ref)

    def attend(k, _):
        at = pl.ds(pl.multiple_of(k * SLOTS, SLOTS), SLOTS)
        query, key = x_ref[at, 0:DH], x_ref[at, DH : 2 * DH]
        value, grad = x_ref[at, 2 * DH : 3 * DH], x_ref[at, 3 * DH : 4 * DH]
        filled = fill_ref[pl.ds(k, 1), :]
        outs, grad_queries = [], []
        for i in range(SLOTS // DH):
            top, width = slice(i * DH, (i + 1) * DH), (i + 1) * DH
            scores = dot(query[top], key[:width], 1, 1) * scaling
            visible = (iota((DH, width), 1) <= iota((DH, width), 0) + i * DH) & (
                filled[:, :width] > 0.5
            )
            scores = jnp.where(visible, scores, NEGATIVE)
            weights = jnp.exp(scores - jnp.max(scores, axis=1, keepdims=True))
            attention = weights * (1.0 / jnp.sum(weights, axis=1, keepdims=True))
            rounded = attention.astype(jnp.bfloat16)
            p_ref[top, :width] = rounded
            outs.append(dot(rounded, value[:width], 1, 0))
            grad_weights = dot(grad[top], value[:width], 1, 1)
            delta = jnp.sum(attention * grad_weights, axis=1, keepdims=True)
            grad_scores = (attention * (grad_weights - delta)).astype(jnp.bfloat16)
            s_ref[top, :width] = grad_scores
            grad_queries.append(dot(grad_scores, key[:width], 1, 0) * scaling)
        y_ref[at, 0:DH] = jnp.concatenate(outs, axis=0).astype(jnp.bfloat16)
        y_ref[at, DH : 2 * DH] = jnp.concatenate(grad_queries, axis=0).astype(jnp.bfloat16)
        grad_key = dot(s_ref[...], query, 0, 0) * scaling
        y_ref[at, 2 * DH : 3 * DH] = grad_key.astype(jnp.bfloat16)
        y_ref[at, 3 * DH : 4 * DH] = dot(p_ref[...], grad, 0, 0).astype(jnp.bfloat16)
        key_ref[k] = key
        wide = key.astype(jnp.float32)
        square_ref[pl.ds(k, 1), :] = lax.dot_general(
            jnp.ones((8, DH), jnp.float32),
            wide * wide,
            (((1,), (1,)), ((), ())),
            precision=lax.Precision.HIGHEST,
            preferred_element_type=jnp.float32,
        )[0:1]
        return 0

    lax.fori_loop(0, OWN, attend, 0)

    def gather(g, _):
        pieces = [
            y_ref[pl.ds(pl.multiple_of(k * SLOTS + g * PIECE, 16), PIECE), :] for k in range(OWN)
        ]
        block = dot(chosen(g), jnp.concatenate(pieces, axis=0), 1, 0)
        out_ref[pl.ds(pl.multiple_of(g * part, part), part), :] = block.astype(jnp.bfloat16)
        return 0

    lax.fori_loop(0, GROUPS, gather, 0)


def attention(places, filled, block, rows):
    vmem = pl.BlockSpec(memory_space=pltpu.VMEM)
    return pl.pallas_call(
        functools.partial(attention_kernel, rows),
        in_specs=[vmem] * 3,
        out_specs=[vmem] * 3,
        out_shape=[
            jax.ShapeDtypeStruct(block.shape, jnp.bfloat16),
            jax.ShapeDtypeStruct((OWN, SLOTS, DH), jnp.bfloat16),
            jax.ShapeDtypeStruct((OWN, SLOTS), jnp.float32),
        ],
        scratch_shapes=[
            pltpu.VMEM((OWN * SLOTS, 4 * DH), jnp.bfloat16),
            pltpu.VMEM((OWN * SLOTS, 4 * DH), jnp.bfloat16),
            pltpu.VMEM((SLOTS, SLOTS), jnp.bfloat16),
            pltpu.VMEM((SLOTS, SLOTS), jnp.bfloat16),
        ],
        compiler_params=pltpu.CompilerParams(vmem_limit_bytes=VMEM),
        name="attention",
    )(places, filled, block)


def exchange(x, axis):
    return lax.all_to_all(x, axis, 0, 0, tiled=True)


def share(x, axis):
    return exchange(jnp.broadcast_to(x[None], (lax.axis_size(axis),) + x.shape), axis)


def body(queries, keys, values, d_out, cluster_id):
    seq = lax.axis_index("seq")
    member = (cluster_id == iota((1, CLUSTERS), 1)).astype(jnp.int32)
    running = jnp.cumsum(member, axis=0)
    ordinal = jnp.sum((running - 1) * member, axis=1, keepdims=True)
    own_counts = jnp.sum(member, axis=0)
    counts = share(own_counts[None].astype(jnp.float32), "seq")[:, 0].astype(jnp.int32)

    totals = jnp.sum(counts, axis=0)
    index = jnp.arange(CLUSTERS, dtype=jnp.int32)
    before = (totals[None, :] > totals[:, None]) | (
        (totals[None, :] == totals[:, None]) & (index[None, :] < index[:, None])
    )
    rank = jnp.sum(before.astype(jnp.int32), axis=1)
    turn = rank // N_SEQ
    owner = jnp.where(turn % 2 == 0, rank % N_SEQ, N_SEQ - 1 - rank % N_SEQ)
    same = owner[None, :] == owner[:, None]
    pair = jnp.sum(jnp.where(same[None], counts[:, None, :], 0), axis=2)
    earlier = same & (turn[None, :] < turn[:, None])
    start = jnp.sum(jnp.where(earlier[None], counts[:, None, :], 0), axis=2)
    mine = (owner[None, :] == seq) & (turn[None, :] == jnp.arange(OWN, dtype=jnp.int32)[:, None])
    here_counts = jnp.sum(jnp.where(mine[:, None, :], counts[None], 0), axis=2)
    here_start = jnp.sum(jnp.where(mine[:, None, :], start[None], 0), axis=2)
    start_me = lax.dynamic_index_in_dim(start, seq, 0, keepdims=False)

    def with_rows(rows, queries, keys, values, d_out):
        table = owner * rows + start_me
        place = ordinal + jnp.sum(member * table[None, :], axis=1, keepdims=True)
        sent = pack(place.reshape(1, -1), (queries, keys, values, d_out), rows)
        slot = jnp.arange(CAPC, dtype=jnp.int32)
        taken = slot[None, None, :] < here_counts[:, :, None]
        line = (jnp.arange(N_SEQ, dtype=jnp.int32) % GROUP) * rows
        spot = here_start[:, :, None] + slot[None, None, :] + line[None, :, None]
        spot = jnp.where(taken, spot, -1).reshape(OWN, GROUPS, PIECE)
        spot = spot.transpose(1, 0, 2).reshape(GROUPS, OWN * PIECE)
        filled = taken.reshape(OWN, SLOTS).astype(jnp.float32)
        received = exchange(sent.reshape(N_SEQ, rows, 4 * DH), "seq")
        results, key_rows, squares = attention(
            spot, filled, received.reshape(N_SEQ * rows, 4 * DH), rows
        )
        returned = exchange(results.reshape(N_SEQ, rows, 4 * DH), "seq")
        norm = jnp.sum(share(squares, "head"), axis=0)
        size = jnp.sum(here_counts, axis=1).astype(jnp.float32)
        unit = filled / jnp.sqrt(norm / D + EPSILON)
        means = jnp.sum(unit[:, :, None] * key_rows.astype(jnp.float32), axis=1) / size[:, None]
        spread = jnp.sum(share(jnp.sum(means * means, axis=1)[None], "head"), axis=0)[0]
        rows_here = means / jnp.sqrt(spread / D + EPSILON)[:, None]
        rows_all = share(rows_here, "seq").reshape(CLUSTERS, DH)
        centroids = rows_all[owner * OWN + turn]
        outs = unpack(place, returned.reshape(N_SEQ * rows, 4 * DH))
        return (*outs, centroids)

    return lax.cond(
        jnp.max(pair) <= ROWS_SHORT,
        functools.partial(with_rows, ROWS_SHORT),
        functools.partial(with_rows, ROWS_FULL),
        queries,
        keys,
        values,
        d_out,
    )


def solution(mesh):
    wide = P("seq", "head")
    return jax.shard_map(
        body,
        mesh=mesh,
        in_specs=(wide, wide, wide, wide, P("seq", None)),
        out_specs=(wide, wide, wide, wide, P(None, "head")),
        check_vma=False,
    )
```

time: 812 us -> 395 us (0.49)
  the two profiles are of different devices: /device:TPU:32 before, /device:TPU:2 now
where the time goes in v1:
time: 395 us; the launch traced here: 394 us
  waiting for transfers between devices  248 us (63%)
  Pallas kernels  45.8 us (12%)
  starting transfers between devices  37.5 us (9%)
  blocking collectives  33.4 us (8%)
  other arithmetic  15.1 us (4%)
  local copies, waits for them, and re-layouts  12 us (3%)
    all_to_all x4, waiting for transfers between devices, exchange(): return lax.all_to_all(x, axis, 0, 0, tiled=True)  248 us
    all_to_all x4, starting transfers between devices, exchange(): return lax.all_to_all(x, axis, 0, 0, tiled=True)  37.5 us
    all_to_all x2, blocking collectives, exchange(): return lax.all_to_all(x, axis, 0, 0, tiled=True)  33.4 us
    pallas_call x1, Pallas kernels, attention(): pl.pallas_call(functools.partial(attention_kernel, rows), in_specs=[vmem]...  27.1 us
    pallas_call x1, Pallas kernels, unpack(): pl.pallas_call(unpack_kernel, grid=(tokens // tile,), in_specs=[pl.BlockS...  10 us
    pallas_call x1, Pallas kernels, pack(): pl.pallas_call(pack_kernel, grid=(GROUPS,), in_specs=[pl.BlockSpec((1, to...  8.67 us
  transfers between devices with their start and end apart: 4, of which 4 were waited for; matrix products, arithmetic and copies ran while one was open for 4% of the time, Pallas kernels for 0%

profile of v1, /device:TPU:2, one launch (start us, length us, event | category | flops | bytes accessed | tf_op | source)
XLA Modules:
  0.0 394.1 jit_solution(8452533046972764050)
XLA Ops:
  0.6 1.1 convert_reduce_fusion
  2.4 15.5 %all-to-all-start.10 = ((f32[32,1,256]{2,1,0:T(1,128)}), f32[32,1,256]{2,1,0:T(1,128)S(1)}, u32[]{:S(2)}, u32[]{:S(2)}) async-start(f32[32,1,256]{2,1,0:T(1,128)} %broadcast_in_dim.114), calls=%async_computation.10 | async-start | bytes 65536 | tf_op jit(solution)/shard_map/all_to_all | solution.py:188
  19.4 1.3 copy-done
  20.7 3.2 add_add_fusion
  24.0 4.2 %copy.48 = s32[256,16,128]{0,2,1:T(8,128)} copy(s32[256,16,128]{0,1,2:T(8,128)} %add_add_fusion) | data formatting | bytes 4194304 | tf_op jit(solution)/shard_map/sub | solution.py:199
  28.2 2.7 all-to-all-done.10
  31.4 2.3 select_reduce_fusion.6
  35.0 359.0 %conditional.1 = (bf16[2048,128]{1,0:T(8,128)(2,1)}, bf16[2048,128]{1,0:T(8,128)(2,1)}, bf16[2048,128]{1,0:T(8,128)(2,1)}, bf16[2048,128]{1,0:T(8,128)(2,1)}, f32[256,128]{1,0:T(8,128)}) conditional(s32[]{:T(128)} %convert_element_type.67, (s32[256]{0:T(256)S(1)}, s32[32,256]{1,0:T(8,128)S(1)}, s32[2048,256]{1,0:T(8,128)S(1)}, ...), branch_computations={%region_11.18_spmd, %region_18.25_spmd} | conditional | flops 3616691 | bytes 33190550 | solution.py:247
  35.3 2.3 select_reduce_fusion.3
  38.3 8.7 %pack.3 = bf16[2560,512]{1,0:T(8,128)(2,1)} custom-call(s32[1,2048]{1,0:T(1,128)} %bitcast.43, bf16[2048,128]{1,0:T(8,128)(2,1)S(1)} %get-tuple-element.129.q_ref, bf16[2048,128]{1,0:T(8,128)(2,1)S(1)} %copy-done.3, bf16[2048,128]{1,0:T(8,128)(2,1)S(1)} %copy-done.5, bf16[2048,128]{1,0:T(8,128)(2,1)S(1)} %copy-done.7), custom_call_target="tpu_custom_call" | custom-call | tf_op jit(solution)/shard_map/cond/branch_1_fun/pack/pallas_call | solution.py:55
  46.9 9.6 %all-to-all-start.5 = ((bf16[32,80,512]{2,1,0:T(8,128)(2,1)}), bf16[32,80,512]{2,1,0:T(8,128)(2,1)}, u32[]{:S(2)}, u32[]{:S(2)}) async-start(bf16[32,80,512]{2,1,0:T(8,128)(2,1)} %bitcast.35), calls=%async_computation.5 | async-start | bytes 5242880 | tf_op jit(solution)/shard_map/cond/branch_1_fun/all_to_all | solution.py:188
  59.1 117.7 %all-to-all-done.5 = bf16[32,80,512]{2,1,0:T(8,128)(2,1)} async-done(((bf16[32,80,512]{2,1,0:T(8,128)(2,1)}), bf16[32,80,512]{2,1,0:T(8,128)(2,1)}, u32[]{:S(2)}, u32[]{:S(2)}) %all-to-all-start.5) | async-done | bytes 2621472 | tf_op jit(solution)/shard_map/cond/branch_1_fun/all_to_all | solution.py:188
  176.8 27.1 %attention.3 = (bf16[2560,512]{1,0:T(8,128)(2,1)}, bf16[8,384,128]{2,1,0:T(8,128)(2,1)}, f32[8,384]{1,0:T(8,128)}) custom-call(s32[8,384]{1,0:T(8,128)} %reshape.466.place_ref, f32[8,384]{1,0:T(8,128)} %get-tuple-element.170.fill_ref, bf16[2560,512]{1,0:T(8,128)(2,1)} %bitcast.14.in_ref), custom_call_target="tpu_custom_call" | custom-call | tf_op jit(solution)/shard_map/cond/branch_1_fun/attention/pallas_call | solution.py:167
  203.9 1.4 broadcast_in_dim.76
  205.3 7.5 %all-to-all-start.7 = ((f32[16,8,384]{2,1,0:T(8,128)}), f32[16,8,384]{2,1,0:T(8,128)S(1)}, u32[]{:S(2)}, u32[]{:S(2)}) async-start(f32[16,8,384]{2,1,0:T(8,128)} %broadcast_in_dim.76), calls=%async_computation.7 | async-start | bytes 393216 | tf_op jit(solution)/shard_map/cond/branch_1_fun/all_to_all | solution.py:188
  212.9 6.9 %all-to-all-done.7 = f32[16,8,384]{2,1,0:T(8,128)S(1)} async-done(((f32[16,8,384]{2,1,0:T(8,128)}), f32[16,8,384]{2,1,0:T(8,128)S(1)}, u32[]{:S(2)}, u32[]{:S(2)}) %all-to-all-start.7) | async-done | bytes 196640 | tf_op jit(solution)/shard_map/cond/branch_1_fun/all_to_all | solution.py:188
  219.8 1.6 multiply_reduce_fusion.4
  221.6 10.5 %all_to_all.47 = f32[16,1,8]{2,1,0:T(1,128)S(1)} all-to-all(f32[16,1,8]{2,1,0:T(1,128)S(1)} %broadcast_in_dim.77), channel_id=1, replica_groups=mesh['seq'=32,'head'=16] {'head'}, dimensions={0} | all-to-all | bytes 1024 | tf_op jit(solution)/shard_map/cond/branch_1_fun/all_to_all | solution.py:188
  232.3 22.9 %all_to_all.48 = f32[32,8,128]{2,1,0:T(8,128)S(1)} all-to-all(f32[32,8,128]{2,1,0:T(8,128)S(1)} %broadcast_in_dim.78), channel_id=1, replica_groups=mesh['seq'=32,'head'=16] {'seq'}, dimensions={0} | all-to-all | bytes 262144 | tf_op jit(solution)/shard_map/cond/branch_1_fun/all_to_all | solution.py:188
  255.2 4.9 %all-to-all-start.6 = ((bf16[32,80,512]{2,1,0:T(8,128)(2,1)}), bf16[32,80,512]{2,1,0:T(8,128)(2,1)}, u32[]{:S(2)}, u32[]{:S(2)}) async-start(bf16[32,80,512]{2,1,0:T(8,128)(2,1)} %bitcast.37), calls=%async_computation.6 | async-start | bytes 5242880 | tf_op jit(solution)/shard_map/cond/branch_1_fun/all_to_all | solution.py:188
  260.2 1.4 copy.45.place_ref
  261.6 1.3 gather_fusion.1
  262.9 121.2 %all-to-all-done.6 = bf16[32,80,512]{2,1,0:T(8,128)(2,1)} async-done(((bf16[32,80,512]{2,1,0:T(8,128)(2,1)}), bf16[32,80,512]{2,1,0:T(8,128)(2,1)}, u32[]{:S(2)}, u32[]{:S(2)}) %all-to-all-start.6) | async-done | bytes 2621472 | tf_op jit(solution)/shard_map/cond/branch_1_fun/all_to_all | solution.py:188
  384.1 10.0 %unpack.3 = (bf16[2048,128]{1,0:T(8,128)(2,1)}, bf16[2048,128]{1,0:T(8,128)(2,1)}, bf16[2048,128]{1,0:T(8,128)(2,1)}, bf16[2048,128]{1,0:T(8,128)(2,1)}) custom-call(s32[2048,1]{1,0:T(8,128)} %copy.45.place_ref, bf16[2560,512]{1,0:T(8,128)(2,1)} %bitcast.16.in_ref), custom_call_target="tpu_custom_call" | custom-call | tf_op jit(solution)/shard_map/cond/branch_1_fun/unpack/pallas_call | solution.py:78
  (62 shorter events, 7.0 us)
Async XLA Ops:
  0.6 18.3 %copy-start.10 = (s32[2048,1]{0,1:T(1,128)S(1)}, s32[2048,1]{0,1:T(1,128)}, u32[]{:S(2)}) copy-start(s32[2048,1]{0,1:T(1,128)} %param.11) | copy-start | bytes 24580
  2.4 28.5 %all-to-all-start.10 = ((f32[32,1,256]{2,1,0:T(1,128)}), f32[32,1,256]{2,1,0:T(1,128)S(1)}, u32[]{:S(2)}, u32[]{:S(2)}) async-start(f32[32,1,256]{2,1,0:T(1,128)} %broadcast_in_dim.114), calls=%async_computation.10 | async-start | bytes 65536 | tf_op jit(solution)/shard_map/all_to_all | solution.py:188
  19.4 1.3 copy-start
  24.0 11.1 %copy-start.1 = (bf16[2048,128]{1,0:T(8,128)(2,1)S(1)}, bf16[2048,128]{1,0:T(8,128)(2,1)}, u32[]{:S(2)}) copy-start(bf16[2048,128]{1,0:T(8,128)(2,1)} %param.7) | copy-start | bytes 1572868
  35.3 3.0 copy-start.3
  35.3 3.0 copy-start.5
  35.3 2.9 copy-start.7
  46.9 129.9 %all-to-all-start.5 = ((bf16[32,80,512]{2,1,0:T(8,128)(2,1)}), bf16[32,80,512]{2,1,0:T(8,128)(2,1)}, u32[]{:S(2)}, u32[]{:S(2)}) async-start(bf16[32,80,512]{2,1,0:T(8,128)(2,1)} %bitcast.35), calls=%async_computation.5 | async-start | bytes 5242880 | tf_op jit(solution)/shard_map/cond/branch_1_fun/all_to_all | solution.py:188
  205.3 14.5 %all-to-all-start.7 = ((f32[16,8,384]{2,1,0:T(8,128)}), f32[16,8,384]{2,1,0:T(8,128)S(1)}, u32[]{:S(2)}, u32[]{:S(2)}) async-start(f32[16,8,384]{2,1,0:T(8,128)} %broadcast_in_dim.76), calls=%async_computation.7 | async-start | bytes 393216 | tf_op jit(solution)/shard_map/cond/branch_1_fun/all_to_all | solution.py:188
  255.2 5.0 %copy-start.9 = (s32[2048]{0:T(1024)S(1)}, s32[2048]{0:T(1024)}, u32[]{:S(2)}) copy-start(s32[2048]{0:T(1024)} %add.195) | copy-start | bytes 24580 | tf_op jit(solution)/shard_map/cond
  255.2 128.9 %all-to-all-start.6 = ((bf16[32,80,512]{2,1,0:T(8,128)(2,1)}), bf16[32,80,512]{2,1,0:T(8,128)(2,1)}, u32[]{:S(2)}, u32[]{:S(2)}) async-start(bf16[32,80,512]{2,1,0:T(8,128)(2,1)} %bitcast.37), calls=%async_computation.6 | async-start | bytes 5242880 | tf_op jit(solution)/shard_map/cond/branch_1_fun/all_to_all | solution.py:188

commit v2 on v1

v2 whole, which is shorter than its diff:
```python
import functools

import jax
import jax.numpy as jnp
from jax import lax
from jax.experimental import pallas as pl
from jax.experimental.pallas import tpu as pltpu
from jax.sharding import PartitionSpec as P

DH = 128
CLUSTERS = 256
CAPC = 12
D = 2048
N_SEQ = 32
OWN = CLUSTERS // N_SEQ
SLOTS = N_SEQ * CAPC
GROUP = 4
GROUPS = N_SEQ // GROUP
PIECE = GROUP * CAPC
ROWS_SHORT = 72
ROWS_FULL = OWN * CAPC
EPSILON = 1e-06
HIDDEN = 1e30
LOG2E = 1.4426950408889634
TOGETHER = 4
VMEM = 24 * 1024 * 1024
VMEM_MOST = 60 * 1024 * 1024


def iota(shape, dim):
    return lax.broadcasted_iota(jnp.int32, shape, dim)


def one_hot(mask):
    return jnp.where(mask, 1.0, 0.0).astype(jnp.bfloat16)


def dot(a, b, ca, cb):
    return lax.dot_general(a, b, (((ca,), (cb,)), ((), ())), preferred_element_type=jnp.float32)


def pack_kernel(
    rows, seq_ref, plan_ref, cluster_ref, ordinal_ref, q_ref, k_ref, v_ref, g_ref,
    out_ref, place_ref, all_ref, part_ref, sem_ref,
):
    step = pl.program_id(0)
    part = GROUP * rows

    @pl.when(step == 0)
    def _():
        for i, ref in enumerate((q_ref, k_ref, v_ref, g_ref)):
            all_ref[:, i * DH : (i + 1) * DH] = ref[...]
        chosen = (iota((N_SEQ, CLUSTERS), 0) == seq_ref[0, 0])
        start = jnp.sum(jnp.where(chosen, plan_ref[:N_SEQ], 0.0), axis=0, keepdims=True)
        owner = plan_ref[N_SEQ : N_SEQ + 1]
        table = jnp.where(iota((8, CLUSTERS), 0) == 0, owner, start).astype(jnp.bfloat16)
        tokens = cluster_ref.shape[1]
        member = one_hot(iota((CLUSTERS, tokens), 0) == cluster_ref[...])
        found = dot(table, member, 1, 0)
        place = found[0:1] * rows + found[1:2]
        place_ref[...] = place.astype(jnp.int32) + ordinal_ref[...]

    def copy(slot, at):
        return pltpu.make_async_copy(
            part_ref.at[slot], out_ref.at[pl.ds(pl.multiple_of(at * part, part), part)], sem_ref.at[slot]
        )

    slot = lax.rem(step, 2)

    @pl.when(step >= 2)
    def _():
        copy(slot, step - 2).wait()

    wanted = iota((part, place_ref.shape[1]), 0) + step * part
    part_ref[slot] = dot(one_hot(wanted == place_ref[...]), all_ref[...], 1, 0).astype(jnp.bfloat16)
    copy(slot, step).start()

    @pl.when(step == GROUPS - 1)
    def _():
        copy(1 - slot, step - 1).wait()
        copy(slot, step).wait()


def pack(seq, planned, cluster_row, ordinal_row, arrays, rows):
    tokens = cluster_row.shape[1]

    def whole(*shape):
        return pl.BlockSpec(shape, lambda i: (0, 0))

    return pl.pallas_call(
        functools.partial(pack_kernel, rows),
        grid=(GROUPS,),
        in_specs=[
            pl.BlockSpec(memory_space=pltpu.SMEM),
            whole(*planned.shape),
            whole(1, tokens),
            whole(1, tokens),
        ]
        + [whole(tokens, DH)] * 4,
        out_specs=[pl.BlockSpec(memory_space=pltpu.HBM), whole(1, tokens)],
        out_shape=[
            jax.ShapeDtypeStruct((N_SEQ * rows, 4 * DH), jnp.bfloat16),
            jax.ShapeDtypeStruct((1, tokens), jnp.int32),
        ],
        scratch_shapes=[
            pltpu.VMEM((tokens, 4 * DH), jnp.bfloat16),
            pltpu.VMEM((2, GROUP * rows, 4 * DH), jnp.bfloat16),
            pltpu.SemaphoreType.DMA((2,)),
        ],
        compiler_params=pltpu.CompilerParams(vmem_limit_bytes=VMEM_MOST),
        name="pack",
    )(seq, planned, cluster_row, ordinal_row, *arrays)


def unpack_kernel(place_ref, in_ref, *out_refs):
    tokens = place_ref.shape[0]
    chosen = one_hot(place_ref[...] == iota((tokens, in_ref.shape[0]), 1))
    rows = dot(chosen, in_ref[...], 1, 0).astype(jnp.bfloat16)
    for i, ref in enumerate(out_refs):
        ref[...] = rows[:, i * DH : (i + 1) * DH]


def unpack(place_column, block):
    tokens = place_column.shape[0]
    tile = 256
    return pl.pallas_call(
        unpack_kernel,
        grid=(tokens // tile,),
        in_specs=[
            pl.BlockSpec((tile, 1), lambda i: (i, 0)),
            pl.BlockSpec(block.shape, lambda i: (0, 0)),
        ],
        out_specs=[pl.BlockSpec((tile, DH), lambda i: (i, 0))] * 4,
        out_shape=[jax.ShapeDtypeStruct((tokens, DH), jnp.bfloat16)] * 4,
        compiler_params=pltpu.CompilerParams(vmem_limit_bytes=VMEM),
        name="unpack",
    )(place_column, block)


def attention_kernel(rows, place_ref, in_ref, out_ref, x_ref, hide_ref, y_ref):
    part = GROUP * rows
    scaling = DH**-0.5

    def chosen(g):
        return one_hot(iota((part, OWN * PIECE), 0) == place_ref[pl.ds(g, 1), :])

    def spread(g, _):
        block = in_ref[pl.ds(pl.multiple_of(g * part, part), part), :]
        block = jnp.concatenate([block, jnp.ones((part, DH), jnp.bfloat16)], axis=1)
        full = dot(chosen(g), block, 0, 0)
        moved = full[:, : 4 * DH].astype(jnp.bfloat16)
        hide = (full[:, 4 * DH :] - 1.0) * HIDDEN
        for k in range(OWN):
            at = pl.ds(pl.multiple_of(k * SLOTS + g * PIECE, 16), PIECE)
            x_ref[at, :] = moved[k * PIECE : (k + 1) * PIECE]
            hide_ref[at, :] = hide[k * PIECE : (k + 1) * PIECE]
        return 0

    lax.fori_loop(0, GROUPS, spread, 0)
    causal = iota((DH, DH), 0) <= iota((DH, DH), 1)

    def attend(k):
        at = pl.ds(pl.multiple_of(k * SLOTS, SLOTS), SLOTS)
        query, key = x_ref[at, 0:DH], x_ref[at, DH : 2 * DH]
        value, grad = x_ref[at, 2 * DH : 3 * DH], x_ref[at, 3 * DH : 4 * DH]
        hide = hide_ref[at, :]
        weights_all, changes_all = [], []
        for i in range(SLOTS // DH):
            low, high = i * DH, (i + 1) * DH
            scores = dot(key[:high], query[low:high], 1, 1) * (scaling * LOG2E) + hide[:high]
            last = jnp.where(causal, scores[low:], -HIDDEN)
            scores = last if i == 0 else jnp.concatenate([scores[:low], last], axis=0)
            weights = jnp.exp2(scores - jnp.max(scores, axis=0, keepdims=True))
            attention = weights * (1.0 / jnp.sum(weights, axis=0, keepdims=True))
            grad_weights = dot(value[:high], grad[low:high], 1, 1)
            delta = jnp.sum(attention * grad_weights, axis=0, keepdims=True)
            weights_all.append(attention.astype(jnp.bfloat16))
            changes_all.append((attention * (grad_weights - delta)).astype(jnp.bfloat16))
        outs, grad_queries = [], []
        for i in range(SLOTS // DH):
            high = (i + 1) * DH
            outs.append(dot(weights_all[i], value[:high], 0, 0))
            grad_queries.append(dot(changes_all[i], key[:high], 0, 0) * scaling)
        grad_values, grad_keys = [], []
        for j in range(SLOTS // DH):
            row = slice(j * DH, (j + 1) * DH)
            rest = slice(j * DH, SLOTS)
            wide = jnp.concatenate([w[row] for w in weights_all[j:]], axis=1)
            grad_values.append(dot(wide, grad[rest], 1, 0))
            wide = jnp.concatenate([c[row] for c in changes_all[j:]], axis=1)
            grad_keys.append(dot(wide, query[rest], 1, 0) * scaling)
        for i, pieces in enumerate((outs, grad_queries, grad_keys, grad_values)):
            y_ref[at, i * DH : (i + 1) * DH] = jnp.concatenate(pieces, axis=0).astype(jnp.bfloat16)

    def attend_several(i, _):
        for j in range(TOGETHER):
            attend(i * TOGETHER + j)
        return 0

    lax.fori_loop(0, OWN // TOGETHER, attend_several, 0)

    def gather(g, _):
        pieces = [
            y_ref[pl.ds(pl.multiple_of(k * SLOTS + g * PIECE, 16), PIECE), :] for k in range(OWN)
        ]
        block = dot(chosen(g), jnp.concatenate(pieces, axis=0), 1, 0)
        out_ref[pl.ds(pl.multiple_of(g * part, part), part), :] = block.astype(jnp.bfloat16)
        return 0

    lax.fori_loop(0, GROUPS, gather, 0)


def attention(places, block, rows):
    vmem = pl.BlockSpec(memory_space=pltpu.VMEM)
    return pl.pallas_call(
        functools.partial(attention_kernel, rows),
        in_specs=[vmem] * 2,
        out_specs=vmem,
        out_shape=jax.ShapeDtypeStruct(block.shape, jnp.bfloat16),
        scratch_shapes=[
            pltpu.VMEM((OWN * SLOTS, 4 * DH), jnp.bfloat16),
            pltpu.VMEM((OWN * SLOTS, DH), jnp.float32),
            pltpu.VMEM((OWN * SLOTS, 4 * DH), jnp.bfloat16),
        ],
        compiler_params=pltpu.CompilerParams(vmem_limit_bytes=VMEM),
        name="attention",
    )(places, block)


def across(x, step):
    low = (iota(x.shape, 1) & step) == 0
    return jnp.where(low, pltpu.roll(x, x.shape[1] - step, 1), pltpu.roll(x, step, 1))


def plan_kernel(counts_ref, out_ref, most_ref):
    counts = counts_ref[...]
    size_row = jnp.sum(counts, axis=0, keepdims=True)
    size_column = dot(counts.astype(jnp.bfloat16), jnp.ones((N_SEQ, CLUSTERS), jnp.bfloat16), 0, 0)
    square = (CLUSTERS, CLUSTERS)
    before = (size_column > size_row) | (
        (size_column == size_row) & (iota(square, 0) < iota(square, 1))
    )
    rank = jnp.sum(jnp.where(before, 1.0, 0.0), axis=0, keepdims=True).astype(jnp.int32)
    turn, spot = lax.shift_right_logical(rank, 5), rank & (N_SEQ - 1)
    owner = jnp.where((turn & 1) == 0, spot, N_SEQ - 1 - spot)
    number = iota((8, CLUSTERS), 1).astype(jnp.float32)
    named = jnp.concatenate([counts, number], axis=0).astype(jnp.bfloat16)
    tables = []
    for k in range(OWN):
        here = jnp.where(turn == k, owner, -1)
        tables.append(dot(named, one_hot(iota((DH, CLUSTERS), 0) == here), 1, 1))
    load = functools.reduce(jnp.add, [t[:N_SEQ] for t in tables])

    def cost(x):
        over = jnp.maximum(x - 60.0, 0.0)
        over = over * over
        return over * over

    for step in (1, 2, 4, 8, 16):
        other = across(load, step)
        for k in range(OWN):
            theirs = across(tables[k], step)
            change = theirs[:N_SEQ] - tables[k][:N_SEQ]
            more, less = load + change, other - change
            gain = (cost(more) + cost(less)) - (cost(load) + cost(other))
            swap = jnp.sum(gain, axis=0, keepdims=True) < 0.0
            load = jnp.where(swap, more, load)
            other = jnp.where(swap, less, other)
            tables[k] = jnp.where(swap, theirs, tables[k])
    owners = iota((N_SEQ, DH), 1)
    load = jnp.where(owners < N_SEQ, load, 0.0)
    most_ref[...] = jnp.max(jnp.max(load, axis=1, keepdims=True), axis=0, keepdims=True)
    start = jnp.zeros((N_SEQ, DH), jnp.float32)
    result = jnp.zeros((N_SEQ + 8, CLUSTERS), jnp.float32)
    for k in range(OWN):
        names = tables[k][N_SEQ : N_SEQ + 1]
        names = jnp.where(owners[:1] < N_SEQ, names, -1.0).astype(jnp.int32)
        extra = jnp.where(iota((8, DH), 0) == 0, iota((8, DH), 1), k).astype(jnp.float32)
        values = jnp.concatenate([start, extra], axis=0).astype(jnp.bfloat16)
        result += dot(values, one_hot(iota((CLUSTERS, DH), 0) == names), 1, 1)
        start = start + tables[k][:N_SEQ]
    out_ref[...] = result


def plan(counts):
    return pl.pallas_call(
        plan_kernel,
        out_shape=[
            jax.ShapeDtypeStruct((N_SEQ + 8, CLUSTERS), jnp.float32),
            jax.ShapeDtypeStruct((1, 1), jnp.float32),
        ],
        compiler_params=pltpu.CompilerParams(vmem_limit_bytes=VMEM),
        name="plan",
    )(counts)


def exchange(x, axis):
    return lax.all_to_all(x, axis, 0, 0, tiled=True)


def share(x, axis):
    return exchange(jnp.broadcast_to(x[None], (lax.axis_size(axis),) + x.shape), axis)


def seq_gather(x, returned):
    swapped = lax.ppermute(x, "seq", [(i, i ^ 1) for i in range(N_SEQ)])
    x = jnp.stack([x, swapped])
    for stride in (1, 4):
        pieces = [x]
        for step in (1, 2, 3):
            away = 2 * stride * step
            pairs = [(i, (i + away) % N_SEQ) for i in range(N_SEQ)]
            pieces.append(lax.ppermute(x, "seq", pairs))
        x = jnp.concatenate(pieces, axis=0)
        if stride == 1:
            x, returned = lax.optimization_barrier((x, returned))
    return x, returned


def body(queries, keys, values, d_out, cluster_id):
    seq = lax.axis_index("seq")
    tokens = queries.shape[0]
    member = (cluster_id == iota((1, CLUSTERS), 1)).astype(jnp.int32)
    own_counts, cluster_id = lax.optimization_barrier((jnp.sum(member, axis=0), cluster_id))
    member = (cluster_id == iota((1, CLUSTERS), 1)).astype(jnp.int32)
    running = jnp.cumsum(member, axis=0)
    ordinal = jnp.sum((running - 1) * member, axis=1)
    counts = share(own_counts[None].astype(jnp.float32), "seq")[:, 0]
    counts, ordinal = lax.optimization_barrier((counts, ordinal))
    planned, most = plan(counts)

    def with_rows(rows, queries, keys, values, d_out):
        sent, place = pack(
            seq.reshape(1, 1),
            planned,
            cluster_id.reshape(1, tokens),
            ordinal.reshape(1, tokens),
            (queries, keys, values, d_out),
            rows,
        )
        received = exchange(sent.reshape(N_SEQ, rows, 4 * DH), "seq")
        plan_whole = planned.astype(jnp.int32)
        start, owner, turn = plan_whole[:N_SEQ], plan_whole[N_SEQ], plan_whole[N_SEQ + 1]
        turns = jnp.arange(OWN, dtype=jnp.int32)
        mine = (owner[None, :] == seq) & (turn[None, :] == turns[:, None])
        here_counts = jnp.sum(jnp.where(mine[:, None, :], counts[None], 0.0), axis=2)
        here_start = jnp.sum(jnp.where(mine[:, None, :], start[None], 0), axis=2)
        slot = jnp.arange(CAPC, dtype=jnp.int32)
        taken = slot[None, None, :] < here_counts.astype(jnp.int32)[:, :, None]
        line = (jnp.arange(N_SEQ, dtype=jnp.int32) % GROUP) * rows
        spot = here_start[:, :, None] + slot[None, None, :] + line[None, :, None]
        spot = jnp.where(taken, spot, -1).reshape(OWN, GROUPS, PIECE)
        spot = spot.transpose(1, 0, 2).reshape(GROUPS, OWN * PIECE)
        spot, place = lax.optimization_barrier((spot, place.reshape(tokens, 1)))
        results = attention(spot, received.reshape(N_SEQ * rows, 4 * DH), rows)
        returned = exchange(results.reshape(N_SEQ, rows, 4 * DH), "seq")
        key_rows = received[:, :, DH : 2 * DH].astype(jnp.float32).reshape(N_SEQ * rows, DH)
        squares = jnp.sum(key_rows * key_rows, axis=1)
        norm = jnp.sum(lax.all_gather(squares, "head"), axis=0)
        row = jnp.arange(rows, dtype=jnp.int32)[None, None, :] - here_start[:, :, None]
        held = (row >= 0) & (row < here_counts.astype(jnp.int32)[:, :, None])
        held = held.reshape(OWN, N_SEQ * rows)
        unit = jnp.where(held, 1.0 / jnp.sqrt(norm / D + EPSILON)[None], 0.0)
        means = jnp.dot(unit, key_rows, precision=lax.Precision.HIGHEST)
        means = means / jnp.sum(here_counts, axis=1)[:, None]
        spread = jnp.sum(means * means, axis=1, keepdims=True)
        spread = lax.optimization_barrier(jnp.broadcast_to(spread, (OWN, DH)))
        spread = jnp.sum(lax.all_gather(spread, "head"), axis=0)
        every, returned = seq_gather(means / jnp.sqrt(spread / D + EPSILON), returned)
        back = lax.rem(N_SEQ // 2 + seq // 2 - owner // 2, N_SEQ // 2)
        entry = back * 2 + ((owner ^ seq) & 1)
        centroids = every.reshape(CLUSTERS, DH)[entry * OWN + turn]
        outs = unpack(place, returned.reshape(N_SEQ * rows, 4 * DH))
        return (*outs, centroids)

    return lax.cond(
        most[0, 0] <= ROWS_SHORT,
        functools.partial(with_rows, ROWS_SHORT),
        functools.partial(with_rows, ROWS_FULL),
        queries,
        keys,
        values,
        d_out,
    )


def solution(mesh):
    wide = P("seq", "head")
    return jax.shard_map(
        body,
        mesh=mesh,
        in_specs=(wide, wide, wide, wide, P("seq", None)),
        out_specs=(wide, wide, wide, wide, P(None, "head")),
        check_vma=False,
    )
```

time: 395 us -> 316 us (0.80)
  the two profiles are of different devices: /device:TPU:2 before, /device:TPU:30 now
where the time goes in v2:
time: 316 us; the launch traced here: 315 us
  waiting for transfers between devices  168 us (53%)
  starting transfers between devices  56.6 us (18%)
  blocking collectives  44.5 us (14%)
  Pallas kernels  33.2 us (11%)
  local copies, waits for them, and re-layouts  6.89 us (2%)
  other arithmetic  3.79 us (1%)
    all_to_all x3, waiting for transfers between devices, exchange(): return lax.all_to_all(x, axis, 0, 0, tiled=True)  126 us
    ppermute x6, waiting for transfers between devices, seq_gather(): pieces.append(lax.ppermute(x, 'seq', pairs))  40.1 us
    ppermute x6, starting transfers between devices, seq_gather(): pieces.append(lax.ppermute(x, 'seq', pairs))  30.3 us
    all_to_all x3, starting transfers between devices, exchange(): return lax.all_to_all(x, axis, 0, 0, tiled=True)  24.3 us
    all_gather x1, blocking collectives, with_rows(): spread = jnp.sum(lax.all_gather(spread, 'head'), axis=0)  23 us
    all_gather x1, blocking collectives, with_rows(): norm = jnp.sum(lax.all_gather(squares, 'head'), axis=0)  21.5 us
    pallas_call x1, Pallas kernels, attention(): pl.pallas_call(functools.partial(attention_kernel, rows), in_specs=[vmem]...  11.9 us
    pallas_call x1, Pallas kernels, pack(): pl.pallas_call(functools.partial(pack_kernel, rows), grid=(GROUPS,), in_s...  9.53 us
  transfers between devices with their start and end apart: 10, of which 6 were waited for; matrix products, arithmetic and copies ran while one was open for 2% of the time, Pallas kernels for 3%

profile of v2, /device:TPU:30, one launch (start us, length us, event | category | flops | bytes accessed | tf_op | source)
XLA Modules:
  0.0 315.5 jit_solution(13472012626077944228)
XLA Ops:
  2.3 15.5 %all-to-all-start.4 = ((f32[32,1,256]{2,1,0:T(1,128)}), f32[32,1,256]{2,1,0:T(1,128)S(1)}, u32[]{:S(2)}, u32[]{:S(2)}) async-start(f32[32,1,256]{2,1,0:T(1,128)} %broadcast_in_dim.144), calls=%async_computation.4 | async-start | bytes 65536 | tf_op jit(solution)/shard_map/all_to_all | solution.py:298
  21.5 9.4 %all-to-all-done.4 = f32[32,1,256]{2,1,0:T(1,128)S(1)} async-done(((f32[32,1,256]{2,1,0:T(1,128)}), f32[32,1,256]{2,1,0:T(1,128)S(1)}, u32[]{:S(2)}, u32[]{:S(2)}) %all-to-all-start.4) | async-done | bytes 32800 | tf_op jit(solution)/shard_map/all_to_all | solution.py:298
  30.8 2.7 plan.1
  34.2 281.3 %conditional.1 = (bf16[2048,128]{1,0:T(8,128)(2,1)}, bf16[2048,128]{1,0:T(8,128)(2,1)}, bf16[2048,128]{1,0:T(8,128)(2,1)}, bf16[2048,128]{1,0:T(8,128)(2,1)}, f32[256,128]{1,0:T(8,128)}) conditional(s32[]{:T(128)} %bitcast.42, (f32[40,256]{1,0:T(8,128)S(1)}, s32[]{:T(128)}, f32[32,256]{1,0:T(8,128)S(1)}, s32[2048,1]{0,1:T(1,128)S(1)}, ...), branch_computations={%region_4.12_spmd, %region_12.20_spmd} | conditional | flops 39585808 | bytes 35313348 | solution.py:376
  34.4 9.5 %pack.3 = (bf16[2304,512]{1,0:T(8,128)(2,1)}, s32[1,2048]{1,0:T(1,128)}) custom-call(s32[1,1]{1,0:T(1,128)} %bitcast.20.seq_ref, f32[40,256]{1,0:T(8,128)S(1)} %get-tuple-element.55.plan_ref, s32[1,2048]{1,0:T(1,128)S(1)} %bitcast.118, s32[1,2048]{1,0:T(1,128)S(1)} %bitcast.120, bf16[2048,128]{1,0:T(8,128)(2,1)S(1)} %get-tuple-element.101.q_ref, ...), custom_call_target="tpu_custom_call" | custom-call | tf_op jit(solution)/shard_map/cond/branch_1_fun/pack/pallas_call | solution.py:90
  44.0 4.1 %all-to-all-start.2 = ((bf16[32,72,512]{2,1,0:T(8,128)(2,1)}), bf16[32,72,512]{2,1,0:T(8,128)(2,1)S(1)}, u32[]{:S(2)}, u32[]{:S(2)}) async-start(bf16[32,72,512]{2,1,0:T(8,128)(2,1)} %bitcast.110), calls=%async_computation.2 | async-start | bytes 4718592 | tf_op jit(solution)/shard_map/cond/branch_1_fun/all_to_all | solution.py:298
  49.3 111.5 %all-to-all-done.2 = bf16[32,72,512]{2,1,0:T(8,128)(2,1)S(1)} async-done(((bf16[32,72,512]{2,1,0:T(8,128)(2,1)}), bf16[32,72,512]{2,1,0:T(8,128)(2,1)S(1)}, u32[]{:S(2)}, u32[]{:S(2)}) %all-to-all-start.2) | async-done | bytes 2359328 | tf_op jit(solution)/shard_map/cond/branch_1_fun/all_to_all | solution.py:298
  160.8 11.9 %attention.3 = bf16[2304,512]{1,0:T(8,128)(2,1)S(1)} custom-call(s32[8,384]{1,0:T(8,128)S(1)} %reshape.528.place_ref, bf16[2304,512]{1,0:T(8,128)(2,1)S(1)} %bitcast.107), custom_call_target="tpu_custom_call" | custom-call | tf_op jit(solution)/shard_map/cond/branch_1_fun/attention/pallas_call | solution.py:215
  172.7 1.4 copy-done.1
  174.0 4.8 %all-to-all-start.3 = ((bf16[32,72,512]{2,1,0:T(8,128)(2,1)}), bf16[32,72,512]{2,1,0:T(8,128)(2,1)}, u32[]{:S(2)}, u32[]{:S(2)}) async-start(bf16[32,72,512]{2,1,0:T(8,128)(2,1)} %bitcast.108), calls=%async_computation.3 | async-start | bytes 4718592 | tf_op jit(solution)/shard_map/cond/branch_1_fun/all_to_all | solution.py:298
  179.7 21.5 %all-gather.3 = f32[16,1,2304]{2,1,0:T(1,128)S(1)} all-gather(f32[1,1,2304]{2,1,0:T(1,128)S(1)} %reshape.561), channel_id=1, replica_groups=mesh['seq'=32,'head'=16] {'head'}, dimensions={0}, use_global_device_ids=true | all-gather | bytes 156672 | tf_op jit(solution)/shard_map/cond/branch_1_fun/all_gather | solution.py:359
  202.4 23.0 %all-gather.1 = f32[128,128]{1,0:T(8,128)S(1)} all-gather(f32[8,128]{1,0:T(8,128)S(1)} %broadcast_in_dim.142), channel_id=3, replica_groups=mesh['seq'=32,'head'=16] {'head'}, dimensions={0}, use_global_device_ids=true | all-gather | bytes 69632 | tf_op jit(solution)/shard_map/cond/branch_1_fun/all_gather | solution.py:368
  225.4 1.9 collective-permute-start.7
  228.5 3.5 %collective-permute-start.8 = (f32[2,8,128]{2,1,0:T(8,128)S(1)}, f32[2,8,128]{2,1,0:T(8,128)S(1)}, u32[]{:S(2)}, u32[]{:S(2)}) collective-permute-start(f32[2,8,128]{2,1,0:T(8,128)S(1)} %pad_maximum_fusion.1), channel_id=1, source_target_pairs={{0,32},{16,48},{32,64},{48,80},{64,96},{80,112},{96,128},{112,144}... | collective-permute-start | bytes 24584 | tf_op jit(solution)/shard_map/cond/branch_1_fun/ppermute | solution.py:313
  232.0 4.3 %collective-permute-start.9 = (f32[2,8,128]{2,1,0:T(8,128)S(1)}, f32[2,8,128]{2,1,0:T(8,128)S(1)}, u32[]{:S(2)}, u32[]{:S(2)}) collective-permute-start(f32[2,8,128]{2,1,0:T(8,128)S(1)} %pad_maximum_fusion.1), channel_id=1, source_target_pairs={{0,64},{16,80},{32,96},{48,112},{64,128},{80,144},{96,160},{112,17... | collective-permute-start | bytes 24584 | tf_op jit(solution)/shard_map/cond/branch_1_fun/ppermute | solution.py:313
  236.3 6.4 %collective-permute-start.10 = (f32[2,8,128]{2,1,0:T(8,128)S(1)}, f32[2,8,128]{2,1,0:T(8,128)S(1)}, u32[]{:S(2)}, u32[]{:S(2)}) collective-permute-start(f32[2,8,128]{2,1,0:T(8,128)S(1)} %pad_maximum_fusion.1), channel_id=1, source_target_pairs={{0,96},{16,112},{32,128},{48,144},{64,160},{80,176},{96,192},{112,... | collective-permute-start | bytes 24584 | tf_op jit(solution)/shard_map/cond/branch_1_fun/ppermute | solution.py:313
  242.8 36.5 %collective-permute-done.8 = f32[2,8,128]{2,1,0:T(8,128)S(1)} collective-permute-done((f32[2,8,128]{2,1,0:T(8,128)S(1)}, f32[2,8,128]{2,1,0:T(8,128)S(1)}, u32[]{:S(2)}, u32[]{:S(2)}) %collective-permute-start.8) | collective-permute-done | bytes 8224 | tf_op jit(solution)/shard_map/cond/branch_1_fun/ppermute | solution.py:313
  279.2 3.7 %collective-permute-done.9 = f32[2,8,128]{2,1,0:T(8,128)S(1)} collective-permute-done((f32[2,8,128]{2,1,0:T(8,128)S(1)}, f32[2,8,128]{2,1,0:T(8,128)S(1)}, u32[]{:S(2)}, u32[]{:S(2)}) %collective-permute-start.9) | collective-permute-done | bytes 8224 | tf_op jit(solution)/shard_map/cond/branch_1_fun/ppermute | solution.py:313
  282.9 5.6 %all-to-all-done.3 = bf16[32,72,512]{2,1,0:T(8,128)(2,1)} async-done(((bf16[32,72,512]{2,1,0:T(8,128)(2,1)}), bf16[32,72,512]{2,1,0:T(8,128)(2,1)}, u32[]{:S(2)}, u32[]{:S(2)}) %all-to-all-start.3) | async-done | bytes 2359328 | tf_op jit(solution)/shard_map/cond/branch_1_fun/all_to_all | solution.py:298
  288.5 1.9 collective-permute-start.11
  290.4 10.6 %collective-permute-start.12 = (f32[8,8,128]{2,1,0:T(8,128)S(1)}, f32[8,8,128]{2,1,0:T(8,128)S(1)}, u32[]{:S(2)}, u32[]{:S(2)}) collective-permute-start(f32[8,8,128]{2,1,0:T(8,128)S(1)} %constant_dynamic-update-slice_fusion.5), channel_id=1, source_target_pairs={{0,256},{16,272},{32,288},{48,304},{64,320},{80,336},{96,352},{112... | collective-permute-start | bytes 98312 | tf_op jit(solution)/shard_map/cond/branch_1_fun/ppermute | solution.py:313
  301.0 3.6 %collective-permute-start.13 = (f32[8,8,128]{2,1,0:T(8,128)S(1)}, f32[8,8,128]{2,1,0:T(8,128)S(1)}, u32[]{:S(2)}, u32[]{:S(2)}) collective-permute-start(f32[8,8,128]{2,1,0:T(8,128)S(1)} %constant_dynamic-update-slice_fusion.5), channel_id=1, source_target_pairs={{0,384},{16,400},{32,416},{48,432},{64,448},{80,464},{96,480},{112... | collective-permute-start | bytes 98312 | tf_op jit(solution)/shard_map/cond/branch_1_fun/ppermute | solution.py:313
  305.0 9.1 %unpack.3 = (bf16[2048,128]{1,0:T(8,128)(2,1)}, bf16[2048,128]{1,0:T(8,128)(2,1)}, bf16[2048,128]{1,0:T(8,128)(2,1)}, bf16[2048,128]{1,0:T(8,128)(2,1)}) custom-call(s32[2048,1]{1,0:T(8,128)S(1)} %copy.52.place_ref, bf16[2304,512]{1,0:T(8,128)(2,1)} %bitcast.31.in_ref), custom_call_target="tpu_custom_call" | custom-call | tf_op jit(solution)/shard_map/cond/branch_1_fun/unpack/pallas_call | solution.py:126
  314.1 1.3 gather_fusion.1
  (66 shorter events, 10.0 us)
Async XLA Ops:
  2.3 28.5 %all-to-all-start.4 = ((f32[32,1,256]{2,1,0:T(1,128)}), f32[32,1,256]{2,1,0:T(1,128)S(1)}, u32[]{:S(2)}, u32[]{:S(2)}) async-start(f32[32,1,256]{2,1,0:T(1,128)} %broadcast_in_dim.144), calls=%async_computation.4 | async-start | bytes 65536 | tf_op jit(solution)/shard_map/all_to_all | solution.py:298
  19.3 1.3 copy-start.4
  20.5 13.7 %copy-start.2 = (bf16[2048,128]{1,0:T(8,128)(2,1)S(1)}, bf16[2048,128]{1,0:T(8,128)(2,1)}, u32[]{:S(2)}) copy-start(bf16[2048,128]{1,0:T(8,128)(2,1)} %param.7) | copy-start | bytes 1572868
  20.5 13.7 %copy-start.3 = (bf16[2048,128]{1,0:T(8,128)(2,1)S(1)}, bf16[2048,128]{1,0:T(8,128)(2,1)}, u32[]{:S(2)}) copy-start(bf16[2048,128]{1,0:T(8,128)(2,1)} %param.8) | copy-start | bytes 1572868
  44.0 116.8 %all-to-all-start.2 = ((bf16[32,72,512]{2,1,0:T(8,128)(2,1)}), bf16[32,72,512]{2,1,0:T(8,128)(2,1)S(1)}, u32[]{:S(2)}, u32[]{:S(2)}) async-start(bf16[32,72,512]{2,1,0:T(8,128)(2,1)} %bitcast.110), calls=%async_computation.2 | async-start | bytes 4718592 | tf_op jit(solution)/shard_map/cond/branch_1_fun/all_to_all | solution.py:298
  172.6 1.4 copy-start.1
  174.0 114.5 %all-to-all-start.3 = ((bf16[32,72,512]{2,1,0:T(8,128)(2,1)}), bf16[32,72,512]{2,1,0:T(8,128)(2,1)}, u32[]{:S(2)}, u32[]{:S(2)}) async-start(bf16[32,72,512]{2,1,0:T(8,128)(2,1)} %bitcast.108), calls=%async_computation.3 | async-start | bytes 4718592 | tf_op jit(solution)/shard_map/cond/branch_1_fun/all_to_all | solution.py:298
  178.8 125.8 %copy-start.6 = (s32[1,2048]{1,0:T(1,128)S(1)}, s32[1,2048]{1,0:T(1,128)}, u32[]{:S(2)}) copy-start(s32[1,2048]{1,0:T(1,128)} %get-tuple-element.64) | copy-start | bytes 24580 | tf_op jit(solution)/shard_map/cond
  225.4 3.1 collective-permute-start.7
  228.5 50.7 %collective-permute-start.8 = (f32[2,8,128]{2,1,0:T(8,128)S(1)}, f32[2,8,128]{2,1,0:T(8,128)S(1)}, u32[]{:S(2)}, u32[]{:S(2)}) collective-permute-start(f32[2,8,128]{2,1,0:T(8,128)S(1)} %pad_maximum_fusion.1), channel_id=1, source_target_pairs={{0,32},{16,48},{32,64},{48,80},{64,96},{80,112},{96,128},{112,144}... | collective-permute-start | bytes 24584 | tf_op jit(solution)/shard_map/cond/branch_1_fun/ppermute | solution.py:313
  232.0 50.9 %collective-permute-start.9 = (f32[2,8,128]{2,1,0:T(8,128)S(1)}, f32[2,8,128]{2,1,0:T(8,128)S(1)}, u32[]{:S(2)}, u32[]{:S(2)}) collective-permute-start(f32[2,8,128]{2,1,0:T(8,128)S(1)} %pad_maximum_fusion.1), channel_id=1, source_target_pairs={{0,64},{16,80},{32,96},{48,112},{64,128},{80,144},{96,160},{112,17... | collective-permute-start | bytes 24584 | tf_op jit(solution)/shard_map/cond/branch_1_fun/ppermute | solution.py:313
  236.3 46.6 %collective-permute-start.10 = (f32[2,8,128]{2,1,0:T(8,128)S(1)}, f32[2,8,128]{2,1,0:T(8,128)S(1)}, u32[]{:S(2)}, u32[]{:S(2)}) collective-permute-start(f32[2,8,128]{2,1,0:T(8,128)S(1)} %pad_maximum_fusion.1), channel_id=1, source_target_pairs={{0,96},{16,112},{32,128},{48,144},{64,160},{80,176},{96,192},{112,... | collective-permute-start | bytes 24584 | tf_op jit(solution)/shard_map/cond/branch_1_fun/ppermute | solution.py:313
  288.5 25.6 %collective-permute-start.11 = (f32[8,8,128]{2,1,0:T(8,128)S(1)}, f32[8,8,128]{2,1,0:T(8,128)S(1)}, u32[]{:S(2)}, u32[]{:S(2)}) collective-permute-start(f32[8,8,128]{2,1,0:T(8,128)S(1)} %constant_dynamic-update-slice_fusion.5), channel_id=1, source_target_pairs={{0,128},{16,144},{32,160},{48,176},{64,192},{80,208},{96,224},{112... | collective-permute-start | bytes 98312 | tf_op jit(solution)/shard_map/cond/branch_1_fun/ppermute | solution.py:313
  290.4 23.7 %collective-permute-start.12 = (f32[8,8,128]{2,1,0:T(8,128)S(1)}, f32[8,8,128]{2,1,0:T(8,128)S(1)}, u32[]{:S(2)}, u32[]{:S(2)}) collective-permute-start(f32[8,8,128]{2,1,0:T(8,128)S(1)} %constant_dynamic-update-slice_fusion.5), channel_id=1, source_target_pairs={{0,256},{16,272},{32,288},{48,304},{64,320},{80,336},{96,352},{112... | collective-permute-start | bytes 98312 | tf_op jit(solution)/shard_map/cond/branch_1_fun/ppermute | solution.py:313
  301.0 13.1 %collective-permute-start.13 = (f32[8,8,128]{2,1,0:T(8,128)S(1)}, f32[8,8,128]{2,1,0:T(8,128)S(1)}, u32[]{:S(2)}, u32[]{:S(2)}) collective-permute-start(f32[8,8,128]{2,1,0:T(8,128)S(1)} %constant_dynamic-update-slice_fusion.5), channel_id=1, source_target_pairs={{0,384},{16,400},{32,416},{48,432},{64,448},{80,464},{96,480},{112... | collective-permute-start | bytes 98312 | tf_op jit(solution)/shard_map/cond/branch_1_fun/ppermute | solution.py:313

commit v3 on v2

--- a/solution.py
+++ b/solution.py
@@ -302,7 +302,7 @@
     return exchange(jnp.broadcast_to(x[None], (lax.axis_size(axis),) + x.shape), axis)
 
 
-def seq_gather(x, returned):
+def seq_gather(x):
     swapped = lax.ppermute(x, "seq", [(i, i ^ 1) for i in range(N_SEQ)])
     x = jnp.stack([x, swapped])
     for stride in (1, 4):
@@ -311,10 +311,9 @@
             away = 2 * stride * step
             pairs = [(i, (i + away) % N_SEQ) for i in range(N_SEQ)]
             pieces.append(lax.ppermute(x, "seq", pairs))
-        x = jnp.concatenate(pieces, axis=0)
         if stride == 1:
-            x, returned = lax.optimization_barrier((x, returned))
-    return x, returned
+            x = jnp.concatenate(pieces, axis=0)
+    return pieces
 
 
 def body(queries, keys, values, d_out, cluster_id):
@@ -366,11 +365,13 @@
         spread = jnp.sum(means * means, axis=1, keepdims=True)
         spread = lax.optimization_barrier(jnp.broadcast_to(spread, (OWN, DH)))
         spread = jnp.sum(lax.all_gather(spread, "head"), axis=0)
-        every, returned = seq_gather(means / jnp.sqrt(spread / D + EPSILON), returned)
+        pieces = seq_gather(means / jnp.sqrt(spread / D + EPSILON))
         back = lax.rem(N_SEQ // 2 + seq // 2 - owner // 2, N_SEQ // 2)
         entry = back * 2 + ((owner ^ seq) & 1)
-        centroids = every.reshape(CLUSTERS, DH)[entry * OWN + turn]
         outs = unpack(place, returned.reshape(N_SEQ * rows, 4 * DH))
+        pieces, outs = lax.optimization_barrier((pieces, outs))
+        every = jnp.concatenate(pieces, axis=0).reshape(CLUSTERS, DH)
+        centroids = every[entry * OWN + turn]
         return (*outs, centroids)
 
     return lax.cond(

time: 316 us -> 316 us (level)
  waiting for transfers between devices: 168 us -> 162 us
  starting transfers between devices: 56.6 us -> 62.2 us
    all_to_all x3, waiting for transfers between devices: 126 us -> 121 us  [exchange(): return lax.all_to_all(x, axis, 0, 0, tiled=True)]
    ppermute x6, starting transfers between devices: 30.3 us -> 35.9 us  [seq_gather(): pieces.append(lax.ppermute(x, 'seq', pairs))]
  transfers between devices with their start and end apart: 10 -> 10, of which waited for: 6 -> 5; matrix products, arithmetic and copies ran while one was open for 2% -> 2% of each run, Pallas kernels for 3% -> 3%
where the time goes in v3:
time: 316 us; the launch traced here: 315 us
  waiting for transfers between devices  162 us (51%)
  starting transfers between devices  62.2 us (20%)
  blocking collectives  44.5 us (14%)
  Pallas kernels  33.2 us (11%)
  local copies, waits for them, and re-layouts  6.89 us (2%)
  other arithmetic  3.79 us (1%)
    all_to_all x3, waiting for transfers between devices, exchange(): return lax.all_to_all(x, axis, 0, 0, tiled=True)  121 us
    ppermute x6, waiting for transfers between devices, seq_gather(): pieces.append(lax.ppermute(x, 'seq', pairs))  40.1 us
    ppermute x6, starting transfers between devices, seq_gather(): pieces.append(lax.ppermute(x, 'seq', pairs))  35.9 us
    all_to_all x3, starting transfers between devices, exchange(): return lax.all_to_all(x, axis, 0, 0, tiled=True)  24.3 us
    all_gather x1, blocking collectives, with_rows(): spread = jnp.sum(lax.all_gather(spread, 'head'), axis=0)  23 us
    all_gather x1, blocking collectives, with_rows(): norm = jnp.sum(lax.all_gather(squares, 'head'), axis=0)  21.5 us
    pallas_call x1, Pallas kernels, attention(): pl.pallas_call(functools.partial(attention_kernel, rows), in_specs=[vmem]...  11.9 us
    pallas_call x1, Pallas kernels, pack(): pl.pallas_call(functools.partial(pack_kernel, rows), grid=(GROUPS,), in_s...  9.53 us
  transfers between devices with their start and end apart: 10, of which 5 were waited for; matrix products, arithmetic and copies ran while one was open for 2% of the time, Pallas kernels for 3%

profile of v3, /device:TPU:30, one launch (start us, length us, event | category | flops | bytes accessed | tf_op | source)
XLA Modules:
  0.0 315.5 jit_solution(3402297891118304654)
XLA Ops:
  2.3 15.5 %all-to-all-start.4 = ((f32[32,1,256]{2,1,0:T(1,128)}), f32[32,1,256]{2,1,0:T(1,128)S(1)}, u32[]{:S(2)}, u32[]{:S(2)}) async-start(f32[32,1,256]{2,1,0:T(1,128)} %broadcast_in_dim.144), calls=%async_computation.4 | async-start | bytes 65536 | tf_op jit(solution)/shard_map/all_to_all | solution.py:298
  19.3 1.2 copy.54
  21.5 9.4 %all-to-all-done.4 = f32[32,1,256]{2,1,0:T(1,128)S(1)} async-done(((f32[32,1,256]{2,1,0:T(1,128)}), f32[32,1,256]{2,1,0:T(1,128)S(1)}, u32[]{:S(2)}, u32[]{:S(2)}) %all-to-all-start.4) | async-done | bytes 32800 | tf_op jit(solution)/shard_map/all_to_all | solution.py:298
  30.8 2.7 plan.1
  34.2 281.3 %conditional.1 = (bf16[2048,128]{1,0:T(8,128)(2,1)}, bf16[2048,128]{1,0:T(8,128)(2,1)}, bf16[2048,128]{1,0:T(8,128)(2,1)}, bf16[2048,128]{1,0:T(8,128)(2,1)}, f32[256,128]{1,0:T(8,128)}) conditional(s32[]{:T(128)} %bitcast.42, (f32[40,256]{1,0:T(8,128)S(1)}, s32[]{:T(128)}, f32[32,256]{1,0:T(8,128)S(1)}, s32[2048,1]{0,1:T(1,128)S(1)}, ...), branch_computations={%region_4.12_spmd, %region_12.20_spmd} | conditional | flops 39585808 | bytes 35313348 | solution.py:377
  34.4 9.5 %pack.3 = (bf16[2304,512]{1,0:T(8,128)(2,1)}, s32[1,2048]{1,0:T(1,128)}) custom-call(s32[1,1]{1,0:T(1,128)} %bitcast.19.seq_ref, f32[40,256]{1,0:T(8,128)S(1)} %get-tuple-element.61.plan_ref, s32[1,2048]{1,0:T(1,128)S(1)} %bitcast.118, s32[1,2048]{1,0:T(1,128)S(1)} %bitcast.120, bf16[2048,128]{1,0:T(8,128)(2,1)S(1)} %get-tuple-element.113.q_ref, ...), custom_call_target="tpu_custom_call" | custom-call | tf_op jit(solution)/shard_map/cond/branch_1_fun/pack/pallas_call | solution.py:90
  44.0 4.1 %all-to-all-start.2 = ((bf16[32,72,512]{2,1,0:T(8,128)(2,1)}), bf16[32,72,512]{2,1,0:T(8,128)(2,1)S(1)}, u32[]{:S(2)}, u32[]{:S(2)}) async-start(bf16[32,72,512]{2,1,0:T(8,128)(2,1)} %bitcast.110), calls=%async_computation.2 | async-start | bytes 4718592 | tf_op jit(solution)/shard_map/cond/branch_1_fun/all_to_all | solution.py:298
  49.3 111.5 %all-to-all-done.2 = bf16[32,72,512]{2,1,0:T(8,128)(2,1)S(1)} async-done(((bf16[32,72,512]{2,1,0:T(8,128)(2,1)}), bf16[32,72,512]{2,1,0:T(8,128)(2,1)S(1)}, u32[]{:S(2)}, u32[]{:S(2)}) %all-to-all-start.2) | async-done | bytes 2359328 | tf_op jit(solution)/shard_map/cond/branch_1_fun/all_to_all | solution.py:298
  160.7 11.9 %attention.3 = bf16[2304,512]{1,0:T(8,128)(2,1)S(1)} custom-call(s32[8,384]{1,0:T(8,128)S(1)} %reshape.532.place_ref, bf16[2304,512]{1,0:T(8,128)(2,1)S(1)} %bitcast.107), custom_call_target="tpu_custom_call" | custom-call | tf_op jit(solution)/shard_map/cond/branch_1_fun/attention/pallas_call | solution.py:215
  172.7 1.4 copy-done.1
  174.0 4.8 %all-to-all-start.3 = ((bf16[32,72,512]{2,1,0:T(8,128)(2,1)}), bf16[32,72,512]{2,1,0:T(8,128)(2,1)}, u32[]{:S(2)}, u32[]{:S(2)}) async-start(bf16[32,72,512]{2,1,0:T(8,128)(2,1)} %bitcast.108), calls=%async_computation.3 | async-start | bytes 4718592 | tf_op jit(solution)/shard_map/cond/branch_1_fun/all_to_all | solution.py:298
  179.7 21.5 %all-gather.3 = f32[16,1,2304]{2,1,0:T(1,128)S(1)} all-gather(f32[1,1,2304]{2,1,0:T(1,128)S(1)} %reshape.561), channel_id=1, replica_groups=mesh['seq'=32,'head'=16] {'head'}, dimensions={0}, use_global_device_ids=true | all-gather | bytes 156672 | tf_op jit(solution)/shard_map/cond/branch_1_fun/all_gather | solution.py:358
  202.4 23.0 %all-gather.1 = f32[128,128]{1,0:T(8,128)S(1)} all-gather(f32[8,128]{1,0:T(8,128)S(1)} %broadcast_in_dim.141), channel_id=3, replica_groups=mesh['seq'=32,'head'=16] {'head'}, dimensions={0}, use_global_device_ids=true | all-gather | bytes 69632 | tf_op jit(solution)/shard_map/cond/branch_1_fun/all_gather | solution.py:367
  225.4 1.9 collective-permute-start.7
  228.5 3.5 %collective-permute-start.8 = (f32[2,8,128]{2,1,0:T(8,128)S(1)}, f32[2,8,128]{2,1,0:T(8,128)S(1)}, u32[]{:S(2)}, u32[]{:S(2)}) collective-permute-start(f32[2,8,128]{2,1,0:T(8,128)S(1)} %pad_maximum_fusion.1), channel_id=1, source_target_pairs={{0,32},{16,48},{32,64},{48,80},{64,96},{80,112},{96,128},{112,144}... | collective-permute-start | bytes 24584 | tf_op jit(solution)/shard_map/cond/branch_1_fun/ppermute | solution.py:313
  232.0 4.3 %collective-permute-start.9 = (f32[2,8,128]{2,1,0:T(8,128)S(1)}, f32[2,8,128]{2,1,0:T(8,128)S(1)}, u32[]{:S(2)}, u32[]{:S(2)}) collective-permute-start(f32[2,8,128]{2,1,0:T(8,128)S(1)} %pad_maximum_fusion.1), channel_id=1, source_target_pairs={{0,64},{16,80},{32,96},{48,112},{64,128},{80,144},{96,160},{112,17... | collective-permute-start | bytes 24584 | tf_op jit(solution)/shard_map/cond/branch_1_fun/ppermute | solution.py:313
  236.3 6.4 %collective-permute-start.10 = (f32[2,8,128]{2,1,0:T(8,128)S(1)}, f32[2,8,128]{2,1,0:T(8,128)S(1)}, u32[]{:S(2)}, u32[]{:S(2)}) collective-permute-start(f32[2,8,128]{2,1,0:T(8,128)S(1)} %pad_maximum_fusion.1), channel_id=1, source_target_pairs={{0,96},{16,112},{32,128},{48,144},{64,160},{80,176},{96,192},{112,... | collective-permute-start | bytes 24584 | tf_op jit(solution)/shard_map/cond/branch_1_fun/ppermute | solution.py:313
  242.8 36.5 %collective-permute-done.8 = f32[2,8,128]{2,1,0:T(8,128)S(1)} collective-permute-done((f32[2,8,128]{2,1,0:T(8,128)S(1)}, f32[2,8,128]{2,1,0:T(8,128)S(1)}, u32[]{:S(2)}, u32[]{:S(2)}) %collective-permute-start.8) | collective-permute-done | bytes 8224 | tf_op jit(solution)/shard_map/cond/branch_1_fun/ppermute | solution.py:313
  279.2 3.7 %collective-permute-done.9 = f32[2,8,128]{2,1,0:T(8,128)S(1)} collective-permute-done((f32[2,8,128]{2,1,0:T(8,128)S(1)}, f32[2,8,128]{2,1,0:T(8,128)S(1)}, u32[]{:S(2)}, u32[]{:S(2)}) %collective-permute-start.9) | collective-permute-done | bytes 8224 | tf_op jit(solution)/shard_map/cond/branch_1_fun/ppermute | solution.py:313
  282.9 6.2 %collective-permute-start.11 = (f32[8,8,128]{2,1,0:T(8,128)S(1)}, f32[8,8,128]{2,1,0:T(8,128)S(1)}, u32[]{:S(2)}, u32[]{:S(2)}) collective-permute-start(f32[8,8,128]{2,1,0:T(8,128)S(1)} %constant_dynamic-update-slice_fusion.5), channel_id=1, source_target_pairs={{0,128},{16,144},{32,160},{48,176},{64,192},{80,208},{96,224},{112... | collective-permute-start | bytes 98312 | tf_op jit(solution)/shard_map/cond/branch_1_fun/ppermute | solution.py:313
  289.1 9.1 %collective-permute-start.12 = (f32[8,8,128]{2,1,0:T(8,128)S(1)}, f32[8,8,128]{2,1,0:T(8,128)S(1)}, u32[]{:S(2)}, u32[]{:S(2)}) collective-permute-start(f32[8,8,128]{2,1,0:T(8,128)S(1)} %constant_dynamic-update-slice_fusion.5), channel_id=1, source_target_pairs={{0,256},{16,272},{32,288},{48,304},{64,320},{80,336},{96,352},{112... | collective-permute-start | bytes 98312 | tf_op jit(solution)/shard_map/cond/branch_1_fun/ppermute | solution.py:313
  298.2 6.4 %collective-permute-start.13 = (f32[8,8,128]{2,1,0:T(8,128)S(1)}, f32[8,8,128]{2,1,0:T(8,128)S(1)}, u32[]{:S(2)}, u32[]{:S(2)}) collective-permute-start(f32[8,8,128]{2,1,0:T(8,128)S(1)} %constant_dynamic-update-slice_fusion.5), channel_id=1, source_target_pairs={{0,384},{16,400},{32,416},{48,432},{64,448},{80,464},{96,480},{112... | collective-permute-start | bytes 98312 | tf_op jit(solution)/shard_map/cond/branch_1_fun/ppermute | solution.py:313
  305.0 9.1 %unpack.3 = (bf16[2048,128]{1,0:T(8,128)(2,1)}, bf16[2048,128]{1,0:T(8,128)(2,1)}, bf16[2048,128]{1,0:T(8,128)(2,1)}, bf16[2048,128]{1,0:T(8,128)(2,1)}) custom-call(s32[2048,1]{1,0:T(8,128)S(1)} %copy.52.place_ref, bf16[2304,512]{1,0:T(8,128)(2,1)} %bitcast.31.in_ref), custom_call_target="tpu_custom_call" | custom-call | tf_op jit(solution)/shard_map/cond/branch_1_fun/unpack/pallas_call | solution.py:126
  314.1 1.3 gather_fusion.1
  (66 shorter events, 8.8 us)
Async XLA Ops:
  2.3 28.5 %all-to-all-start.4 = ((f32[32,1,256]{2,1,0:T(1,128)}), f32[32,1,256]{2,1,0:T(1,128)S(1)}, u32[]{:S(2)}, u32[]{:S(2)}) async-start(f32[32,1,256]{2,1,0:T(1,128)} %broadcast_in_dim.144), calls=%async_computation.4 | async-start | bytes 65536 | tf_op jit(solution)/shard_map/all_to_all | solution.py:298
  19.3 1.3 copy-start.4
  20.5 13.7 %copy-start.2 = (bf16[2048,128]{1,0:T(8,128)(2,1)S(1)}, bf16[2048,128]{1,0:T(8,128)(2,1)}, u32[]{:S(2)}) copy-start(bf16[2048,128]{1,0:T(8,128)(2,1)} %param.7) | copy-start | bytes 1572868
  20.5 13.7 %copy-start.3 = (bf16[2048,128]{1,0:T(8,128)(2,1)S(1)}, bf16[2048,128]{1,0:T(8,128)(2,1)}, u32[]{:S(2)}) copy-start(bf16[2048,128]{1,0:T(8,128)(2,1)} %param.8) | copy-start | bytes 1572868
  44.0 116.8 %all-to-all-start.2 = ((bf16[32,72,512]{2,1,0:T(8,128)(2,1)}), bf16[32,72,512]{2,1,0:T(8,128)(2,1)S(1)}, u32[]{:S(2)}, u32[]{:S(2)}) async-start(bf16[32,72,512]{2,1,0:T(8,128)(2,1)} %bitcast.110), calls=%async_computation.2 | async-start | bytes 4718592 | tf_op jit(solution)/shard_map/cond/branch_1_fun/all_to_all | solution.py:298
  172.6 1.4 copy-start.1
  174.0 131.0 %all-to-all-start.3 = ((bf16[32,72,512]{2,1,0:T(8,128)(2,1)}), bf16[32,72,512]{2,1,0:T(8,128)(2,1)}, u32[]{:S(2)}, u32[]{:S(2)}) async-start(bf16[32,72,512]{2,1,0:T(8,128)(2,1)} %bitcast.108), calls=%async_computation.3 | async-start | bytes 4718592 | tf_op jit(solution)/shard_map/cond/branch_1_fun/all_to_all | solution.py:298
  178.8 125.8 %copy-start.6 = (s32[1,2048]{1,0:T(1,128)S(1)}, s32[1,2048]{1,0:T(1,128)}, u32[]{:S(2)}) copy-start(s32[1,2048]{1,0:T(1,128)} %get-tuple-element.71) | copy-start | bytes 24580 | tf_op jit(solution)/shard_map/cond
  225.4 3.1 collective-permute-start.7
  228.5 50.7 %collective-permute-start.8 = (f32[2,8,128]{2,1,0:T(8,128)S(1)}, f32[2,8,128]{2,1,0:T(8,128)S(1)}, u32[]{:S(2)}, u32[]{:S(2)}) collective-permute-start(f32[2,8,128]{2,1,0:T(8,128)S(1)} %pad_maximum_fusion.1), channel_id=1, source_target_pairs={{0,32},{16,48},{32,64},{48,80},{64,96},{80,112},{96,128},{112,144}... | collective-permute-start | bytes 24584 | tf_op jit(solution)/shard_map/cond/branch_1_fun/ppermute | solution.py:313
  232.0 50.9 %collective-permute-start.9 = (f32[2,8,128]{2,1,0:T(8,128)S(1)}, f32[2,8,128]{2,1,0:T(8,128)S(1)}, u32[]{:S(2)}, u32[]{:S(2)}) collective-permute-start(f32[2,8,128]{2,1,0:T(8,128)S(1)} %pad_maximum_fusion.1), channel_id=1, source_target_pairs={{0,64},{16,80},{32,96},{48,112},{64,128},{80,144},{96,160},{112,17... | collective-permute-start | bytes 24584 | tf_op jit(solution)/shard_map/cond/branch_1_fun/ppermute | solution.py:313
  236.3 46.6 %collective-permute-start.10 = (f32[2,8,128]{2,1,0:T(8,128)S(1)}, f32[2,8,128]{2,1,0:T(8,128)S(1)}, u32[]{:S(2)}, u32[]{:S(2)}) collective-permute-start(f32[2,8,128]{2,1,0:T(8,128)S(1)} %pad_maximum_fusion.1), channel_id=1, source_target_pairs={{0,96},{16,112},{32,128},{48,144},{64,160},{80,176},{96,192},{112,... | collective-permute-start | bytes 24584 | tf_op jit(solution)/shard_map/cond/branch_1_fun/ppermute | solution.py:313
  282.9 31.2 %collective-permute-start.11 = (f32[8,8,128]{2,1,0:T(8,128)S(1)}, f32[8,8,128]{2,1,0:T(8,128)S(1)}, u32[]{:S(2)}, u32[]{:S(2)}) collective-permute-start(f32[8,8,128]{2,1,0:T(8,128)S(1)} %constant_dynamic-update-slice_fusion.5), channel_id=1, source_target_pairs={{0,128},{16,144},{32,160},{48,176},{64,192},{80,208},{96,224},{112... | collective-permute-start | bytes 98312 | tf_op jit(solution)/shard_map/cond/branch_1_fun/ppermute | solution.py:313
  289.1 25.0 %collective-permute-start.12 = (f32[8,8,128]{2,1,0:T(8,128)S(1)}, f32[8,8,128]{2,1,0:T(8,128)S(1)}, u32[]{:S(2)}, u32[]{:S(2)}) collective-permute-start(f32[8,8,128]{2,1,0:T(8,128)S(1)} %constant_dynamic-update-slice_fusion.5), channel_id=1, source_target_pairs={{0,256},{16,272},{32,288},{48,304},{64,320},{80,336},{96,352},{112... | collective-permute-start | bytes 98312 | tf_op jit(solution)/shard_map/cond/branch_1_fun/ppermute | solution.py:313
  298.2 15.9 %collective-permute-start.13 = (f32[8,8,128]{2,1,0:T(8,128)S(1)}, f32[8,8,128]{2,1,0:T(8,128)S(1)}, u32[]{:S(2)}, u32[]{:S(2)}) collective-permute-start(f32[8,8,128]{2,1,0:T(8,128)S(1)} %constant_dynamic-update-slice_fusion.5), channel_id=1, source_target_pairs={{0,384},{16,400},{32,416},{48,432},{64,448},{80,464},{96,480},{112... | collective-permute-start | bytes 98312 | tf_op jit(solution)/shard_map/cond/branch_1_fun/ppermute | solution.py:313

commit v4 on v3

--- a/solution.py
+++ b/solution.py
@@ -20,6 +20,7 @@
 ROWS_SHORT = 72
 ROWS_FULL = OWN * CAPC
 EPSILON = 1e-06
+NEAR = 6
 HIDDEN = 1e30
 LOG2E = 1.4426950408889634
 TOGETHER = 4
@@ -305,15 +306,14 @@
 def seq_gather(x):
     swapped = lax.ppermute(x, "seq", [(i, i ^ 1) for i in range(N_SEQ)])
     x = jnp.stack([x, swapped])
-    for stride in (1, 4):
-        pieces = [x]
-        for step in (1, 2, 3):
-            away = 2 * stride * step
-            pairs = [(i, (i + away) % N_SEQ) for i in range(N_SEQ)]
-            pieces.append(lax.ppermute(x, "seq", pairs))
-        if stride == 1:
-            x = jnp.concatenate(pieces, axis=0)
-    return pieces
+    pieces = [x]
+    for step in range(1, NEAR):
+        pieces.append(far(x, step))
+    return jnp.concatenate(pieces, axis=0)
+
+
+def far(x, chips):
+    return lax.ppermute(x, "seq", [(i, (i + 2 * chips) % N_SEQ) for i in range(N_SEQ)])
 
 
 def body(queries, keys, values, d_out, cluster_id):
@@ -352,8 +352,9 @@
         spot = spot.transpose(1, 0, 2).reshape(GROUPS, OWN * PIECE)
         spot, place = lax.optimization_barrier((spot, place.reshape(tokens, 1)))
         results = attention(spot, received.reshape(N_SEQ * rows, 4 * DH), rows)
+        results, keys_in = lax.optimization_barrier((results, received[:, :, DH : 2 * DH]))
         returned = exchange(results.reshape(N_SEQ, rows, 4 * DH), "seq")
-        key_rows = received[:, :, DH : 2 * DH].astype(jnp.float32).reshape(N_SEQ * rows, DH)
+        key_rows = keys_in.astype(jnp.float32).reshape(N_SEQ * rows, DH)
         squares = jnp.sum(key_rows * key_rows, axis=1)
         norm = jnp.sum(lax.all_gather(squares, "head"), axis=0)
         row = jnp.arange(rows, dtype=jnp.int32)[None, None, :] - here_start[:, :, None]
@@ -365,12 +366,13 @@
         spread = jnp.sum(means * means, axis=1, keepdims=True)
         spread = lax.optimization_barrier(jnp.broadcast_to(spread, (OWN, DH)))
         spread = jnp.sum(lax.all_gather(spread, "head"), axis=0)
-        pieces = seq_gather(means / jnp.sqrt(spread / D + EPSILON))
+        near = seq_gather(means / jnp.sqrt(spread / D + EPSILON))
         back = lax.rem(N_SEQ // 2 + seq // 2 - owner // 2, N_SEQ // 2)
         entry = back * 2 + ((owner ^ seq) & 1)
         outs = unpack(place, returned.reshape(N_SEQ * rows, 4 * DH))
-        pieces, outs = lax.optimization_barrier((pieces, outs))
-        every = jnp.concatenate(pieces, axis=0).reshape(CLUSTERS, DH)
+        near, outs = lax.optimization_barrier((near, outs))
+        pieces = [near] + [far(near, step) for step in range(NEAR, N_SEQ // 2, NEAR)]
+        every = jnp.concatenate(pieces, axis=0).reshape(-1, DH)
         centroids = every[entry * OWN + turn]
         return (*outs, centroids)
 

time: 316 us -> 313 us (level)
  the two profiles are of different devices: /device:TPU:30 before, /device:TPU:18 now
where the time goes in v4:
time: 313 us
  waiting for transfers between devices  162 us (52%)
  starting transfers between devices  61.8 us (20%)
  blocking collectives  43.4 us (14%)
  Pallas kernels  31.5 us (10%)
  local copies, waits for them, and re-layouts  7.02 us (2%)
  other arithmetic  3.8 us (1%)
    all_to_all x3, waiting for transfers between devices, exchange(): return lax.all_to_all(x, axis, 0, 0, tiled=True)  122 us
    ppermute x7, waiting for transfers between devices, far(): lax.ppermute(x, 'seq', [(i, (i + 2 * chips) % N_SEQ) for i in range(N_SEQ)])  39.1 us
    ppermute x7, starting transfers between devices, far(): lax.ppermute(x, 'seq', [(i, (i + 2 * chips) % N_SEQ) for i in range(N_SEQ)])  36.2 us
    all_to_all x3, starting transfers between devices, exchange(): return lax.all_to_all(x, axis, 0, 0, tiled=True)  23.6 us
    all_gather x1, blocking collectives, with_rows(): norm = jnp.sum(lax.all_gather(squares, 'head'), axis=0)  22 us
    all_gather x1, blocking collectives, with_rows(): spread = jnp.sum(lax.all_gather(spread, 'head'), axis=0)  21.4 us
    pallas_call x1, Pallas kernels, attention(): pl.pallas_call(functools.partial(attention_kernel, rows), in_specs=[vmem]...  11.9 us
    pallas_call x1, Pallas kernels, pack(): pl.pallas_call(functools.partial(pack_kernel, rows), grid=(GROUPS,), in_s...  9.53 us
  transfers between devices with their start and end apart: 11, of which 7 were waited for; matrix products, arithmetic and copies ran while one was open for 2% of the time, Pallas kernels for 0%

profile of v4, /device:TPU:18, one launch (start us, length us, event | category | flops | bytes accessed | tf_op | source)
XLA Modules:
  0.0 312.6 jit_solution(12079521309543638201)
XLA Ops:
  2.3 15.5 %all-to-all-start.4 = ((f32[32,1,256]{2,1,0:T(1,128)}), f32[32,1,256]{2,1,0:T(1,128)S(1)}, u32[]{:S(2)}, u32[]{:S(2)}) async-start(f32[32,1,256]{2,1,0:T(1,128)} %broadcast_in_dim.144), calls=%async_computation.4 | async-start | bytes 65536 | tf_op jit(solution)/shard_map/all_to_all | solution.py:299
  21.5 9.4 %all-to-all-done.4 = f32[32,1,256]{2,1,0:T(1,128)S(1)} async-done(((f32[32,1,256]{2,1,0:T(1,128)}), f32[32,1,256]{2,1,0:T(1,128)S(1)}, u32[]{:S(2)}, u32[]{:S(2)}) %all-to-all-start.4) | async-done | bytes 32800 | tf_op jit(solution)/shard_map/all_to_all | solution.py:299
  30.8 2.7 plan.1
  34.2 278.4 %conditional.1 = (bf16[2048,128]{1,0:T(8,128)(2,1)}, bf16[2048,128]{1,0:T(8,128)(2,1)}, bf16[2048,128]{1,0:T(8,128)(2,1)}, bf16[2048,128]{1,0:T(8,128)(2,1)}, f32[256,128]{1,0:T(8,128)}) conditional(s32[]{:T(128)} %bitcast.42, (f32[40,256]{1,0:T(8,128)S(1)}, s32[]{:T(128)}, f32[32,256]{1,0:T(8,128)S(1)}, s32[2048,1]{0,1:T(1,128)S(1)}, ...), branch_computations={%region_4.12_spmd, %region_12.20_spmd} | conditional | flops 39561232 | bytes 37014824 | solution.py:379
  34.4 9.5 %pack.3 = (bf16[2304,512]{1,0:T(8,128)(2,1)}, s32[1,2048]{1,0:T(1,128)}) custom-call(s32[1,1]{1,0:T(1,128)} %bitcast.20.seq_ref, f32[40,256]{1,0:T(8,128)S(1)} %get-tuple-element.60.plan_ref, s32[1,2048]{1,0:T(1,128)S(1)} %bitcast.122, s32[1,2048]{1,0:T(1,128)S(1)} %bitcast.124, bf16[2048,128]{1,0:T(8,128)(2,1)S(1)} %get-tuple-element.111.q_ref, ...), custom_call_target="tpu_custom_call" | custom-call | tf_op jit(solution)/shard_map/cond/branch_1_fun/pack/pallas_call | solution.py:91
  44.0 4.1 %all-to-all-start.2 = ((bf16[32,72,512]{2,1,0:T(8,128)(2,1)}), bf16[32,72,512]{2,1,0:T(8,128)(2,1)S(1)}, u32[]{:S(2)}, u32[]{:S(2)}) async-start(bf16[32,72,512]{2,1,0:T(8,128)(2,1)} %bitcast.114), calls=%async_computation.2 | async-start | bytes 4718592 | tf_op jit(solution)/shard_map/cond/branch_1_fun/all_to_all | solution.py:299
  49.3 111.5 %all-to-all-done.2 = bf16[32,72,512]{2,1,0:T(8,128)(2,1)S(1)} async-done(((bf16[32,72,512]{2,1,0:T(8,128)(2,1)}), bf16[32,72,512]{2,1,0:T(8,128)(2,1)S(1)}, u32[]{:S(2)}, u32[]{:S(2)}) %all-to-all-start.2) | async-done | bytes 2359328 | tf_op jit(solution)/shard_map/cond/branch_1_fun/all_to_all | solution.py:299
  160.7 11.9 %attention.3 = bf16[2304,512]{1,0:T(8,128)(2,1)S(1)} custom-call(s32[8,384]{1,0:T(8,128)S(1)} %reshape.528.place_ref, bf16[2304,512]{1,0:T(8,128)(2,1)S(1)} %bitcast.110), custom_call_target="tpu_custom_call" | custom-call | tf_op jit(solution)/shard_map/cond/branch_1_fun/attention/pallas_call | solution.py:216
  174.2 4.1 %all-to-all-start.3 = ((bf16[32,72,512]{2,1,0:T(8,128)(2,1)}), bf16[32,72,512]{2,1,0:T(8,128)(2,1)S(1)}, u32[]{:S(2)}, u32[]{:S(2)}) async-start(bf16[32,72,512]{2,1,0:T(8,128)(2,1)} %bitcast.112), calls=%async_computation.3 | async-start | bytes 4718592 | tf_op jit(solution)/shard_map/cond/branch_1_fun/all_to_all | solution.py:299
  179.1 22.0 %all-gather.3 = f32[16,1,2304]{2,1,0:T(1,128)S(1)} all-gather(f32[1,1,2304]{2,1,0:T(1,128)S(1)} %reshape.561), channel_id=1, replica_groups=mesh['seq'=32,'head'=16] {'head'}, dimensions={0}, use_global_device_ids=true | all-gather | bytes 156672 | tf_op jit(solution)/shard_map/cond/branch_1_fun/all_gather | solution.py:359
  202.3 21.4 %all-gather.1 = f32[128,128]{1,0:T(8,128)S(1)} all-gather(f32[8,128]{1,0:T(8,128)S(1)} %broadcast_in_dim.142), channel_id=3, replica_groups=mesh['seq'=32,'head'=16] {'head'}, dimensions={0}, use_global_device_ids=true | all-gather | bytes 69632 | tf_op jit(solution)/shard_map/cond/branch_1_fun/all_gather | solution.py:368
  223.8 1.9 collective-permute-start.8
  226.8 3.6 %collective-permute-start.9 = (f32[2,8,128]{2,1,0:T(8,128)S(1)}, f32[2,8,128]{2,1,0:T(8,128)S(1)}, u32[]{:S(2)}, u32[]{:S(2)}) collective-permute-start(f32[2,8,128]{2,1,0:T(8,128)S(1)} %pad_maximum_fusion.1), channel_id=1, source_target_pairs={{0,32},{16,48},{32,64},{48,80},{64,96},{80,112},{96,128},{112,144}... | collective-permute-start | bytes 24584 | tf_op jit(solution)/shard_map/cond/branch_1_fun/ppermute | solution.py:316
  230.4 4.4 %collective-permute-start.10 = (f32[2,8,128]{2,1,0:T(8,128)S(1)}, f32[2,8,128]{2,1,0:T(8,128)S(1)}, u32[]{:S(2)}, u32[]{:S(2)}) collective-permute-start(f32[2,8,128]{2,1,0:T(8,128)S(1)} %pad_maximum_fusion.1), channel_id=1, source_target_pairs={{0,64},{16,80},{32,96},{48,112},{64,128},{80,144},{96,160},{112,17... | collective-permute-start | bytes 24584 | tf_op jit(solution)/shard_map/cond/branch_1_fun/ppermute | solution.py:316
  234.8 6.4 %collective-permute-start.11 = (f32[2,8,128]{2,1,0:T(8,128)S(1)}, f32[2,8,128]{2,1,0:T(8,128)S(1)}, u32[]{:S(2)}, u32[]{:S(2)}) collective-permute-start(f32[2,8,128]{2,1,0:T(8,128)S(1)} %pad_maximum_fusion.1), channel_id=1, source_target_pairs={{0,96},{16,112},{32,128},{48,144},{64,160},{80,176},{96,192},{112,... | collective-permute-start | bytes 24584 | tf_op jit(solution)/shard_map/cond/branch_1_fun/ppermute | solution.py:316
  241.2 5.5 %collective-permute-start.12 = (f32[2,8,128]{2,1,0:T(8,128)S(1)}, f32[2,8,128]{2,1,0:T(8,128)S(1)}, u32[]{:S(2)}, u32[]{:S(2)}) collective-permute-start(f32[2,8,128]{2,1,0:T(8,128)S(1)} %pad_maximum_fusion.1), channel_id=1, source_target_pairs={{0,128},{16,144},{32,160},{48,176},{64,192},{80,208},{96,224},{112... | collective-permute-start | bytes 24584 | tf_op jit(solution)/shard_map/cond/branch_1_fun/ppermute | solution.py:316
  246.7 2.5 collective-permute-start.13
  249.3 29.8 %collective-permute-done.9 = f32[2,8,128]{2,1,0:T(8,128)S(1)} collective-permute-done((f32[2,8,128]{2,1,0:T(8,128)S(1)}, f32[2,8,128]{2,1,0:T(8,128)S(1)}, u32[]{:S(2)}, u32[]{:S(2)}) %collective-permute-start.9) | collective-permute-done | bytes 8224 | tf_op jit(solution)/shard_map/cond/branch_1_fun/ppermute | solution.py:316
  279.1 6.8 %collective-permute-done.10 = f32[2,8,128]{2,1,0:T(8,128)S(1)} collective-permute-done((f32[2,8,128]{2,1,0:T(8,128)S(1)}, f32[2,8,128]{2,1,0:T(8,128)S(1)}, u32[]{:S(2)}, u32[]{:S(2)}) %collective-permute-start.10) | collective-permute-done | bytes 8224 | tf_op jit(solution)/shard_map/cond/branch_1_fun/ppermute | solution.py:316
  286.0 1.6 all-to-all-done.3
  287.6 7.3 %unpack.3 = (bf16[2048,128]{1,0:T(8,128)(2,1)}, bf16[2048,128]{1,0:T(8,128)(2,1)}, bf16[2048,128]{1,0:T(8,128)(2,1)}, bf16[2048,128]{1,0:T(8,128)(2,1)}) custom-call(s32[2048,1]{1,0:T(8,128)S(1)} %copy.52.place_ref, bf16[2304,512]{1,0:T(8,128)(2,1)S(1)} %bitcast.111), custom_call_target="tpu_custom_call" | custom-call | tf_op jit(solution)/shard_map/cond/branch_1_fun/unpack/pallas_call | solution.py:127
  295.0 5.8 %collective-permute-start.14 = (f32[12,8,128]{2,1,0:T(8,128)S(1)}, f32[12,8,128]{2,1,0:T(8,128)S(1)}, u32[]{:S(2)}, u32[]{:S(2)}) collective-permute-start(f32[12,8,128]{2,1,0:T(8,128)S(1)} %constant_dynamic-update-slice_fusion.7), channel_id=1, source_target_pairs={{0,192},{16,208},{32,224},{48,240},{64,256},{80,272},{96,288},{112... | collective-permute-start | bytes 147464 | tf_op jit(solution)/shard_map/cond/branch_1_fun/ppermute | solution.py:316
  300.8 8.0 %collective-permute-start.15 = (f32[12,8,128]{2,1,0:T(8,128)S(1)}, f32[12,8,128]{2,1,0:T(8,128)S(1)}, u32[]{:S(2)}, u32[]{:S(2)}) collective-permute-start(f32[12,8,128]{2,1,0:T(8,128)S(1)} %constant_dynamic-update-slice_fusion.7), channel_id=1, source_target_pairs={{0,384},{16,400},{32,416},{48,432},{64,448},{80,464},{96,480},{112... | collective-permute-start | bytes 147464 | tf_op jit(solution)/shard_map/cond/branch_1_fun/ppermute | solution.py:316
  308.8 2.5 collective-permute-done.15
  (71 shorter events, 12.5 us)
Async XLA Ops:
  2.3 28.5 %all-to-all-start.4 = ((f32[32,1,256]{2,1,0:T(1,128)}), f32[32,1,256]{2,1,0:T(1,128)S(1)}, u32[]{:S(2)}, u32[]{:S(2)}) async-start(f32[32,1,256]{2,1,0:T(1,128)} %broadcast_in_dim.144), calls=%async_computation.4 | async-start | bytes 65536 | tf_op jit(solution)/shard_map/all_to_all | solution.py:299
  19.3 1.3 copy-start.5
  20.5 13.7 %copy-start.3 = (bf16[2048,128]{1,0:T(8,128)(2,1)S(1)}, bf16[2048,128]{1,0:T(8,128)(2,1)}, u32[]{:S(2)}) copy-start(bf16[2048,128]{1,0:T(8,128)(2,1)} %param.7) | copy-start | bytes 1572868
  20.5 13.7 %copy-start.4 = (bf16[2048,128]{1,0:T(8,128)(2,1)S(1)}, bf16[2048,128]{1,0:T(8,128)(2,1)}, u32[]{:S(2)}) copy-start(bf16[2048,128]{1,0:T(8,128)(2,1)} %param.8) | copy-start | bytes 1572868
  44.0 116.8 %all-to-all-start.2 = ((bf16[32,72,512]{2,1,0:T(8,128)(2,1)}), bf16[32,72,512]{2,1,0:T(8,128)(2,1)S(1)}, u32[]{:S(2)}, u32[]{:S(2)}) async-start(bf16[32,72,512]{2,1,0:T(8,128)(2,1)} %bitcast.114), calls=%async_computation.2 | async-start | bytes 4718592 | tf_op jit(solution)/shard_map/cond/branch_1_fun/all_to_all | solution.py:299
  172.6 1.4 copy-start.1
  174.2 113.4 %all-to-all-start.3 = ((bf16[32,72,512]{2,1,0:T(8,128)(2,1)}), bf16[32,72,512]{2,1,0:T(8,128)(2,1)S(1)}, u32[]{:S(2)}, u32[]{:S(2)}) async-start(bf16[32,72,512]{2,1,0:T(8,128)(2,1)} %bitcast.112), calls=%async_computation.3 | async-start | bytes 4718592 | tf_op jit(solution)/shard_map/cond/branch_1_fun/all_to_all | solution.py:299
  178.2 47.5 %copy-start.7 = (s32[1,2048]{1,0:T(1,128)S(1)}, s32[1,2048]{1,0:T(1,128)}, u32[]{:S(2)}) copy-start(s32[1,2048]{1,0:T(1,128)} %get-tuple-element.69) | copy-start | bytes 24580 | tf_op jit(solution)/shard_map/cond
  223.8 3.1 collective-permute-start.8
  226.8 52.3 %collective-permute-start.9 = (f32[2,8,128]{2,1,0:T(8,128)S(1)}, f32[2,8,128]{2,1,0:T(8,128)S(1)}, u32[]{:S(2)}, u32[]{:S(2)}) collective-permute-start(f32[2,8,128]{2,1,0:T(8,128)S(1)} %pad_maximum_fusion.1), channel_id=1, source_target_pairs={{0,32},{16,48},{32,64},{48,80},{64,96},{80,112},{96,128},{112,144}... | collective-permute-start | bytes 24584 | tf_op jit(solution)/shard_map/cond/branch_1_fun/ppermute | solution.py:316
  230.4 55.5 %collective-permute-start.10 = (f32[2,8,128]{2,1,0:T(8,128)S(1)}, f32[2,8,128]{2,1,0:T(8,128)S(1)}, u32[]{:S(2)}, u32[]{:S(2)}) collective-permute-start(f32[2,8,128]{2,1,0:T(8,128)S(1)} %pad_maximum_fusion.1), channel_id=1, source_target_pairs={{0,64},{16,80},{32,96},{48,112},{64,128},{80,144},{96,160},{112,17... | collective-permute-start | bytes 24584 | tf_op jit(solution)/shard_map/cond/branch_1_fun/ppermute | solution.py:316
  234.8 51.1 %collective-permute-start.11 = (f32[2,8,128]{2,1,0:T(8,128)S(1)}, f32[2,8,128]{2,1,0:T(8,128)S(1)}, u32[]{:S(2)}, u32[]{:S(2)}) collective-permute-start(f32[2,8,128]{2,1,0:T(8,128)S(1)} %pad_maximum_fusion.1), channel_id=1, source_target_pairs={{0,96},{16,112},{32,128},{48,144},{64,160},{80,176},{96,192},{112,... | collective-permute-start | bytes 24584 | tf_op jit(solution)/shard_map/cond/branch_1_fun/ppermute | solution.py:316
  241.2 44.7 %collective-permute-start.12 = (f32[2,8,128]{2,1,0:T(8,128)S(1)}, f32[2,8,128]{2,1,0:T(8,128)S(1)}, u32[]{:S(2)}, u32[]{:S(2)}) collective-permute-start(f32[2,8,128]{2,1,0:T(8,128)S(1)} %pad_maximum_fusion.1), channel_id=1, source_target_pairs={{0,128},{16,144},{32,160},{48,176},{64,192},{80,208},{96,224},{112... | collective-permute-start | bytes 24584 | tf_op jit(solution)/shard_map/cond/branch_1_fun/ppermute | solution.py:316
  246.7 39.2 %collective-permute-start.13 = (f32[2,8,128]{2,1,0:T(8,128)S(1)}, f32[2,8,128]{2,1,0:T(8,128)S(1)}, u32[]{:S(2)}, u32[]{:S(2)}) collective-permute-start(f32[2,8,128]{2,1,0:T(8,128)S(1)} %pad_maximum_fusion.1), channel_id=1, source_target_pairs={{0,160},{16,176},{32,192},{48,208},{64,224},{80,240},{96,256},{112... | collective-permute-start | bytes 24584 | tf_op jit(solution)/shard_map/cond/branch_1_fun/ppermute | solution.py:316
  295.0 13.8 %collective-permute-start.14 = (f32[12,8,128]{2,1,0:T(8,128)S(1)}, f32[12,8,128]{2,1,0:T(8,128)S(1)}, u32[]{:S(2)}, u32[]{:S(2)}) collective-permute-start(f32[12,8,128]{2,1,0:T(8,128)S(1)} %constant_dynamic-update-slice_fusion.7), channel_id=1, source_target_pairs={{0,192},{16,208},{32,224},{48,240},{64,256},{80,272},{96,288},{112... | collective-permute-start | bytes 147464 | tf_op jit(solution)/shard_map/cond/branch_1_fun/ppermute | solution.py:316
  300.8 10.5 %collective-permute-start.15 = (f32[12,8,128]{2,1,0:T(8,128)S(1)}, f32[12,8,128]{2,1,0:T(8,128)S(1)}, u32[]{:S(2)}, u32[]{:S(2)}) collective-permute-start(f32[12,8,128]{2,1,0:T(8,128)S(1)} %constant_dynamic-update-slice_fusion.7), channel_id=1, source_target_pairs={{0,384},{16,400},{32,416},{48,432},{64,448},{80,464},{96,480},{112... | collective-permute-start | bytes 147464 | tf_op jit(solution)/shard_map/cond/branch_1_fun/ppermute | solution.py:316

commit v5 on v4

--- a/solution.py
+++ b/solution.py
@@ -23,6 +23,7 @@
 NEAR = 6
 HIDDEN = 1e30
 LOG2E = 1.4426950408889634
+SIDE_BY_SIDE = 4
 TOGETHER = 4
 VMEM = 24 * 1024 * 1024
 VMEM_MOST = 60 * 1024 * 1024
@@ -123,7 +124,7 @@
 
 def unpack(place_column, block):
     tokens = place_column.shape[0]
-    tile = 256
+    tile = 512
     return pl.pallas_call(
         unpack_kernel,
         grid=(tokens // tile,),
@@ -145,6 +146,14 @@
     def chosen(g):
         return one_hot(iota((part, OWN * PIECE), 0) == place_ref[pl.ds(g, 1), :])
 
+    def several(work):
+        def one(i, _):
+            for j in range(SIDE_BY_SIDE):
+                work(i * SIDE_BY_SIDE + j, 0)
+            return 0
+
+        return one
+
     def spread(g, _):
         block = in_ref[pl.ds(pl.multiple_of(g * part, part), part), :]
         block = jnp.concatenate([block, jnp.ones((part, DH), jnp.bfloat16)], axis=1)
@@ -157,7 +166,7 @@
             hide_ref[at, :] = hide[k * PIECE : (k + 1) * PIECE]
         return 0
 
-    lax.fori_loop(0, GROUPS, spread, 0)
+    lax.fori_loop(0, GROUPS // SIDE_BY_SIDE, several(spread), 0)
     causal = iota((DH, DH), 0) <= iota((DH, DH), 1)
 
     def attend(k):
@@ -208,7 +217,7 @@
         out_ref[pl.ds(pl.multiple_of(g * part, part), part), :] = block.astype(jnp.bfloat16)
         return 0
 
-    lax.fori_loop(0, GROUPS, gather, 0)
+    lax.fori_loop(0, GROUPS // SIDE_BY_SIDE, several(gather), 0)
 
 
 def attention(places, block, rows):

time: 313 us -> 310 us (level)
  the two profiles are of different devices: /device:TPU:18 before, /device:TPU:30 now
where the time goes in v5:
time: 310 us; the launch traced here: 309 us
  waiting for transfers between devices  161 us (52%)
  starting transfers between devices  61.7 us (20%)
  blocking collectives  44.5 us (14%)
  Pallas kernels  28.3 us (9%)
  local copies, waits for them, and re-layouts  7.02 us (2%)
  other arithmetic  3.8 us (1%)
    all_to_all x3, waiting for transfers between devices, exchange(): return lax.all_to_all(x, axis, 0, 0, tiled=True)  122 us
    ppermute x7, waiting for transfers between devices, far(): lax.ppermute(x, 'seq', [(i, (i + 2 * chips) % N_SEQ) for i in range(N_SEQ)])  38.1 us
    ppermute x7, starting transfers between devices, far(): lax.ppermute(x, 'seq', [(i, (i + 2 * chips) % N_SEQ) for i in range(N_SEQ)])  36.2 us
    all_to_all x3, starting transfers between devices, exchange(): return lax.all_to_all(x, axis, 0, 0, tiled=True)  23.6 us
    all_gather x1, blocking collectives, with_rows(): spread = jnp.sum(lax.all_gather(spread, 'head'), axis=0)  23 us
    all_gather x1, blocking collectives, with_rows(): norm = jnp.sum(lax.all_gather(squares, 'head'), axis=0)  21.5 us
    pallas_call x1, Pallas kernels, pack(): pl.pallas_call(functools.partial(pack_kernel, rows), grid=(GROUPS,), in_s...  9.53 us
    pallas_call x1, Pallas kernels, attention(): pl.pallas_call(functools.partial(attention_kernel, rows), in_specs=[vmem]...  9.46 us
  transfers between devices with their start and end apart: 11, of which 7 were waited for; matrix products, arithmetic and copies ran while one was open for 2% of the time, Pallas kernels for 0%

profile of v5, /device:TPU:30, one launch (start us, length us, event | category | flops | bytes accessed | tf_op | source)
XLA Modules:
  0.0 309.4 jit_solution(6068405265522198651)
XLA Ops:
  2.3 15.5 %all-to-all-start.4 = ((f32[32,1,256]{2,1,0:T(1,128)}), f32[32,1,256]{2,1,0:T(1,128)S(1)}, u32[]{:S(2)}, u32[]{:S(2)}) async-start(f32[32,1,256]{2,1,0:T(1,128)} %broadcast_in_dim.144), calls=%async_computation.4 | async-start | bytes 65536 | tf_op jit(solution)/shard_map/all_to_all | solution.py:308
  21.5 9.4 %all-to-all-done.4 = f32[32,1,256]{2,1,0:T(1,128)S(1)} async-done(((f32[32,1,256]{2,1,0:T(1,128)}), f32[32,1,256]{2,1,0:T(1,128)S(1)}, u32[]{:S(2)}, u32[]{:S(2)}) %all-to-all-start.4) | async-done | bytes 32800 | tf_op jit(solution)/shard_map/all_to_all | solution.py:308
  30.8 2.7 plan.1
  34.2 275.2 %conditional.1 = (bf16[2048,128]{1,0:T(8,128)(2,1)}, bf16[2048,128]{1,0:T(8,128)(2,1)}, bf16[2048,128]{1,0:T(8,128)(2,1)}, bf16[2048,128]{1,0:T(8,128)(2,1)}, f32[256,128]{1,0:T(8,128)}) conditional(s32[]{:T(128)} %bitcast.42, (f32[40,256]{1,0:T(8,128)S(1)}, s32[]{:T(128)}, f32[32,256]{1,0:T(8,128)S(1)}, s32[2048,1]{0,1:T(1,128)S(1)}, ...), branch_computations={%region_4.12_spmd, %region_12.20_spmd} | conditional | flops 39561232 | bytes 37014824 | solution.py:388
  34.4 9.5 %pack.3 = (bf16[2304,512]{1,0:T(8,128)(2,1)}, s32[1,2048]{1,0:T(1,128)}) custom-call(s32[1,1]{1,0:T(1,128)} %bitcast.20.seq_ref, f32[40,256]{1,0:T(8,128)S(1)} %get-tuple-element.60.plan_ref, s32[1,2048]{1,0:T(1,128)S(1)} %bitcast.122, s32[1,2048]{1,0:T(1,128)S(1)} %bitcast.124, bf16[2048,128]{1,0:T(8,128)(2,1)S(1)} %get-tuple-element.111.q_ref, ...), custom_call_target="tpu_custom_call" | custom-call | tf_op jit(solution)/shard_map/cond/branch_1_fun/pack/pallas_call | solution.py:92
  44.0 4.1 %all-to-all-start.2 = ((bf16[32,72,512]{2,1,0:T(8,128)(2,1)}), bf16[32,72,512]{2,1,0:T(8,128)(2,1)S(1)}, u32[]{:S(2)}, u32[]{:S(2)}) async-start(bf16[32,72,512]{2,1,0:T(8,128)(2,1)} %bitcast.114), calls=%async_computation.2 | async-start | bytes 4718592 | tf_op jit(solution)/shard_map/cond/branch_1_fun/all_to_all | solution.py:308
  49.3 111.5 %all-to-all-done.2 = bf16[32,72,512]{2,1,0:T(8,128)(2,1)S(1)} async-done(((bf16[32,72,512]{2,1,0:T(8,128)(2,1)}), bf16[32,72,512]{2,1,0:T(8,128)(2,1)S(1)}, u32[]{:S(2)}, u32[]{:S(2)}) %all-to-all-start.2) | async-done | bytes 2359328 | tf_op jit(solution)/shard_map/cond/branch_1_fun/all_to_all | solution.py:308
  160.7 9.5 %attention.3 = bf16[2304,512]{1,0:T(8,128)(2,1)S(1)} custom-call(s32[8,384]{1,0:T(8,128)S(1)} %reshape.528.place_ref, bf16[2304,512]{1,0:T(8,128)(2,1)S(1)} %bitcast.110), custom_call_target="tpu_custom_call" | custom-call | tf_op jit(solution)/shard_map/cond/branch_1_fun/attention/pallas_call | solution.py:225
  171.7 4.1 %all-to-all-start.3 = ((bf16[32,72,512]{2,1,0:T(8,128)(2,1)}), bf16[32,72,512]{2,1,0:T(8,128)(2,1)S(1)}, u32[]{:S(2)}, u32[]{:S(2)}) async-start(bf16[32,72,512]{2,1,0:T(8,128)(2,1)} %bitcast.112), calls=%async_computation.3 | async-start | bytes 4718592 | tf_op jit(solution)/shard_map/cond/branch_1_fun/all_to_all | solution.py:308
  176.7 21.5 %all-gather.3 = f32[16,1,2304]{2,1,0:T(1,128)S(1)} all-gather(f32[1,1,2304]{2,1,0:T(1,128)S(1)} %reshape.561), channel_id=1, replica_groups=mesh['seq'=32,'head'=16] {'head'}, dimensions={0}, use_global_device_ids=true | all-gather | bytes 156672 | tf_op jit(solution)/shard_map/cond/branch_1_fun/all_gather | solution.py:368
  199.4 23.0 %all-gather.1 = f32[128,128]{1,0:T(8,128)S(1)} all-gather(f32[8,128]{1,0:T(8,128)S(1)} %broadcast_in_dim.142), channel_id=3, replica_groups=mesh['seq'=32,'head'=16] {'head'}, dimensions={0}, use_global_device_ids=true | all-gather | bytes 69632 | tf_op jit(solution)/shard_map/cond/branch_1_fun/all_gather | solution.py:377
  222.4 1.9 collective-permute-start.8
  225.5 3.6 %collective-permute-start.9 = (f32[2,8,128]{2,1,0:T(8,128)S(1)}, f32[2,8,128]{2,1,0:T(8,128)S(1)}, u32[]{:S(2)}, u32[]{:S(2)}) collective-permute-start(f32[2,8,128]{2,1,0:T(8,128)S(1)} %pad_maximum_fusion.1), channel_id=1, source_target_pairs={{0,32},{16,48},{32,64},{48,80},{64,96},{80,112},{96,128},{112,144}... | collective-permute-start | bytes 24584 | tf_op jit(solution)/shard_map/cond/branch_1_fun/ppermute | solution.py:325
  229.1 4.3 %collective-permute-start.10 = (f32[2,8,128]{2,1,0:T(8,128)S(1)}, f32[2,8,128]{2,1,0:T(8,128)S(1)}, u32[]{:S(2)}, u32[]{:S(2)}) collective-permute-start(f32[2,8,128]{2,1,0:T(8,128)S(1)} %pad_maximum_fusion.1), channel_id=1, source_target_pairs={{0,64},{16,80},{32,96},{48,112},{64,128},{80,144},{96,160},{112,17... | collective-permute-start | bytes 24584 | tf_op jit(solution)/shard_map/cond/branch_1_fun/ppermute | solution.py:325
  233.4 6.4 %collective-permute-start.11 = (f32[2,8,128]{2,1,0:T(8,128)S(1)}, f32[2,8,128]{2,1,0:T(8,128)S(1)}, u32[]{:S(2)}, u32[]{:S(2)}) collective-permute-start(f32[2,8,128]{2,1,0:T(8,128)S(1)} %pad_maximum_fusion.1), channel_id=1, source_target_pairs={{0,96},{16,112},{32,128},{48,144},{64,160},{80,176},{96,192},{112,... | collective-permute-start | bytes 24584 | tf_op jit(solution)/shard_map/cond/branch_1_fun/ppermute | solution.py:325
  239.8 5.5 %collective-permute-start.12 = (f32[2,8,128]{2,1,0:T(8,128)S(1)}, f32[2,8,128]{2,1,0:T(8,128)S(1)}, u32[]{:S(2)}, u32[]{:S(2)}) collective-permute-start(f32[2,8,128]{2,1,0:T(8,128)S(1)} %pad_maximum_fusion.1), channel_id=1, source_target_pairs={{0,128},{16,144},{32,160},{48,176},{64,192},{80,208},{96,224},{112... | collective-permute-start | bytes 24584 | tf_op jit(solution)/shard_map/cond/branch_1_fun/ppermute | solution.py:325
  245.3 2.5 collective-permute-start.13
  247.9 28.8 %collective-permute-done.9 = f32[2,8,128]{2,1,0:T(8,128)S(1)} collective-permute-done((f32[2,8,128]{2,1,0:T(8,128)S(1)}, f32[2,8,128]{2,1,0:T(8,128)S(1)}, u32[]{:S(2)}, u32[]{:S(2)}) %collective-permute-start.9) | collective-permute-done | bytes 8224 | tf_op jit(solution)/shard_map/cond/branch_1_fun/ppermute | solution.py:325
  276.7 6.8 %collective-permute-done.10 = f32[2,8,128]{2,1,0:T(8,128)S(1)} collective-permute-done((f32[2,8,128]{2,1,0:T(8,128)S(1)}, f32[2,8,128]{2,1,0:T(8,128)S(1)}, u32[]{:S(2)}, u32[]{:S(2)}) %collective-permute-start.10) | collective-permute-done | bytes 8224 | tf_op jit(solution)/shard_map/cond/branch_1_fun/ppermute | solution.py:325
  283.5 1.6 all-to-all-done.3
  285.2 6.6 %unpack.3 = (bf16[2048,128]{1,0:T(8,128)(2,1)}, bf16[2048,128]{1,0:T(8,128)(2,1)}, bf16[2048,128]{1,0:T(8,128)(2,1)}, bf16[2048,128]{1,0:T(8,128)(2,1)}) custom-call(s32[2048,1]{1,0:T(8,128)S(1)} %copy.52.place_ref, bf16[2304,512]{1,0:T(8,128)(2,1)S(1)} %bitcast.111), custom_call_target="tpu_custom_call" | custom-call | tf_op jit(solution)/shard_map/cond/branch_1_fun/unpack/pallas_call | solution.py:128
  291.7 5.8 %collective-permute-start.14 = (f32[12,8,128]{2,1,0:T(8,128)S(1)}, f32[12,8,128]{2,1,0:T(8,128)S(1)}, u32[]{:S(2)}, u32[]{:S(2)}) collective-permute-start(f32[12,8,128]{2,1,0:T(8,128)S(1)} %constant_dynamic-update-slice_fusion.7), channel_id=1, source_target_pairs={{0,192},{16,208},{32,224},{48,240},{64,256},{80,272},{96,288},{112... | collective-permute-start | bytes 147464 | tf_op jit(solution)/shard_map/cond/branch_1_fun/ppermute | solution.py:325
  297.5 8.0 %collective-permute-start.15 = (f32[12,8,128]{2,1,0:T(8,128)S(1)}, f32[12,8,128]{2,1,0:T(8,128)S(1)}, u32[]{:S(2)}, u32[]{:S(2)}) collective-permute-start(f32[12,8,128]{2,1,0:T(8,128)S(1)} %constant_dynamic-update-slice_fusion.7), channel_id=1, source_target_pairs={{0,384},{16,400},{32,416},{48,432},{64,448},{80,464},{96,480},{112... | collective-permute-start | bytes 147464 | tf_op jit(solution)/shard_map/cond/branch_1_fun/ppermute | solution.py:325
  305.6 2.5 collective-permute-done.15
  (71 shorter events, 12.5 us)
Async XLA Ops:
  2.3 28.5 %all-to-all-start.4 = ((f32[32,1,256]{2,1,0:T(1,128)}), f32[32,1,256]{2,1,0:T(1,128)S(1)}, u32[]{:S(2)}, u32[]{:S(2)}) async-start(f32[32,1,256]{2,1,0:T(1,128)} %broadcast_in_dim.144), calls=%async_computation.4 | async-start | bytes 65536 | tf_op jit(solution)/shard_map/all_to_all | solution.py:308
  19.3 1.3 copy-start.5
  20.5 13.7 %copy-start.3 = (bf16[2048,128]{1,0:T(8,128)(2,1)S(1)}, bf16[2048,128]{1,0:T(8,128)(2,1)}, u32[]{:S(2)}) copy-start(bf16[2048,128]{1,0:T(8,128)(2,1)} %param.7) | copy-start | bytes 1572868
  20.5 13.7 %copy-start.4 = (bf16[2048,128]{1,0:T(8,128)(2,1)S(1)}, bf16[2048,128]{1,0:T(8,128)(2,1)}, u32[]{:S(2)}) copy-start(bf16[2048,128]{1,0:T(8,128)(2,1)} %param.8) | copy-start | bytes 1572868
  44.0 116.8 %all-to-all-start.2 = ((bf16[32,72,512]{2,1,0:T(8,128)(2,1)}), bf16[32,72,512]{2,1,0:T(8,128)(2,1)S(1)}, u32[]{:S(2)}, u32[]{:S(2)}) async-start(bf16[32,72,512]{2,1,0:T(8,128)(2,1)} %bitcast.114), calls=%async_computation.2 | async-start | bytes 4718592 | tf_op jit(solution)/shard_map/cond/branch_1_fun/all_to_all | solution.py:308
  170.2 1.4 copy-start.1
  171.7 113.4 %all-to-all-start.3 = ((bf16[32,72,512]{2,1,0:T(8,128)(2,1)}), bf16[32,72,512]{2,1,0:T(8,128)(2,1)S(1)}, u32[]{:S(2)}, u32[]{:S(2)}) async-start(bf16[32,72,512]{2,1,0:T(8,128)(2,1)} %bitcast.112), calls=%async_computation.3 | async-start | bytes 4718592 | tf_op jit(solution)/shard_map/cond/branch_1_fun/all_to_all | solution.py:308
  175.8 48.6 %copy-start.7 = (s32[1,2048]{1,0:T(1,128)S(1)}, s32[1,2048]{1,0:T(1,128)}, u32[]{:S(2)}) copy-start(s32[1,2048]{1,0:T(1,128)} %get-tuple-element.69) | copy-start | bytes 24580 | tf_op jit(solution)/shard_map/cond
  222.4 3.1 collective-permute-start.8
  225.5 51.2 %collective-permute-start.9 = (f32[2,8,128]{2,1,0:T(8,128)S(1)}, f32[2,8,128]{2,1,0:T(8,128)S(1)}, u32[]{:S(2)}, u32[]{:S(2)}) collective-permute-start(f32[2,8,128]{2,1,0:T(8,128)S(1)} %pad_maximum_fusion.1), channel_id=1, source_target_pairs={{0,32},{16,48},{32,64},{48,80},{64,96},{80,112},{96,128},{112,144}... | collective-permute-start | bytes 24584 | tf_op jit(solution)/shard_map/cond/branch_1_fun/ppermute | solution.py:325
  229.1 54.4 %collective-permute-start.10 = (f32[2,8,128]{2,1,0:T(8,128)S(1)}, f32[2,8,128]{2,1,0:T(8,128)S(1)}, u32[]{:S(2)}, u32[]{:S(2)}) collective-permute-start(f32[2,8,128]{2,1,0:T(8,128)S(1)} %pad_maximum_fusion.1), channel_id=1, source_target_pairs={{0,64},{16,80},{32,96},{48,112},{64,128},{80,144},{96,160},{112,17... | collective-permute-start | bytes 24584 | tf_op jit(solution)/shard_map/cond/branch_1_fun/ppermute | solution.py:325
  233.4 50.1 %collective-permute-start.11 = (f32[2,8,128]{2,1,0:T(8,128)S(1)}, f32[2,8,128]{2,1,0:T(8,128)S(1)}, u32[]{:S(2)}, u32[]{:S(2)}) collective-permute-start(f32[2,8,128]{2,1,0:T(8,128)S(1)} %pad_maximum_fusion.1), channel_id=1, source_target_pairs={{0,96},{16,112},{32,128},{48,144},{64,160},{80,176},{96,192},{112,... | collective-permute-start | bytes 24584 | tf_op jit(solution)/shard_map/cond/branch_1_fun/ppermute | solution.py:325
  239.8 43.7 %collective-permute-start.12 = (f32[2,8,128]{2,1,0:T(8,128)S(1)}, f32[2,8,128]{2,1,0:T(8,128)S(1)}, u32[]{:S(2)}, u32[]{:S(2)}) collective-permute-start(f32[2,8,128]{2,1,0:T(8,128)S(1)} %pad_maximum_fusion.1), channel_id=1, source_target_pairs={{0,128},{16,144},{32,160},{48,176},{64,192},{80,208},{96,224},{112... | collective-permute-start | bytes 24584 | tf_op jit(solution)/shard_map/cond/branch_1_fun/ppermute | solution.py:325
  245.3 38.2 %collective-permute-start.13 = (f32[2,8,128]{2,1,0:T(8,128)S(1)}, f32[2,8,128]{2,1,0:T(8,128)S(1)}, u32[]{:S(2)}, u32[]{:S(2)}) collective-permute-start(f32[2,8,128]{2,1,0:T(8,128)S(1)} %pad_maximum_fusion.1), channel_id=1, source_target_pairs={{0,160},{16,176},{32,192},{48,208},{64,224},{80,240},{96,256},{112... | collective-permute-start | bytes 24584 | tf_op jit(solution)/shard_map/cond/branch_1_fun/ppermute | solution.py:325
  291.7 13.8 %collective-permute-start.14 = (f32[12,8,128]{2,1,0:T(8,128)S(1)}, f32[12,8,128]{2,1,0:T(8,128)S(1)}, u32[]{:S(2)}, u32[]{:S(2)}) collective-permute-start(f32[12,8,128]{2,1,0:T(8,128)S(1)} %constant_dynamic-update-slice_fusion.7), channel_id=1, source_target_pairs={{0,192},{16,208},{32,224},{48,240},{64,256},{80,272},{96,288},{112... | collective-permute-start | bytes 147464 | tf_op jit(solution)/shard_map/cond/branch_1_fun/ppermute | solution.py:325
  297.5 10.5 %collective-permute-start.15 = (f32[12,8,128]{2,1,0:T(8,128)S(1)}, f32[12,8,128]{2,1,0:T(8,128)S(1)}, u32[]{:S(2)}, u32[]{:S(2)}) collective-permute-start(f32[12,8,128]{2,1,0:T(8,128)S(1)} %constant_dynamic-update-slice_fusion.7), channel_id=1, source_target_pairs={{0,384},{16,400},{32,416},{48,432},{64,448},{80,464},{96,480},{112... | collective-permute-start | bytes 147464 | tf_op jit(solution)/shard_map/cond/branch_1_fun/ppermute | solution.py:325

commit v6 on v5

--- a/solution.py
+++ b/solution.py
@@ -19,6 +19,7 @@
 PIECE = GROUP * CAPC
 ROWS_SHORT = 72
 ROWS_FULL = OWN * CAPC
+PACK_STEPS = 4
 EPSILON = 1e-06
 NEAR = 6
 HIDDEN = 1e30
@@ -46,7 +47,7 @@
     out_ref, place_ref, all_ref, part_ref, sem_ref,
 ):
     step = pl.program_id(0)
-    part = GROUP * rows
+    part = N_SEQ // PACK_STEPS * rows
 
     @pl.when(step == 0)
     def _():
@@ -77,7 +78,7 @@
     part_ref[slot] = dot(one_hot(wanted == place_ref[...]), all_ref[...], 1, 0).astype(jnp.bfloat16)
     copy(slot, step).start()
 
-    @pl.when(step == GROUPS - 1)
+    @pl.when(step == PACK_STEPS - 1)
     def _():
         copy(1 - slot, step - 1).wait()
         copy(slot, step).wait()
@@ -91,7 +92,7 @@
 
     return pl.pallas_call(
         functools.partial(pack_kernel, rows),
-        grid=(GROUPS,),
+        grid=(PACK_STEPS,),
         in_specs=[
             pl.BlockSpec(memory_space=pltpu.SMEM),
             whole(*planned.shape),
@@ -106,7 +107,7 @@
         ],
         scratch_shapes=[
             pltpu.VMEM((tokens, 4 * DH), jnp.bfloat16),
-            pltpu.VMEM((2, GROUP * rows, 4 * DH), jnp.bfloat16),
+            pltpu.VMEM((2, N_SEQ // PACK_STEPS * rows, 4 * DH), jnp.bfloat16),
             pltpu.SemaphoreType.DMA((2,)),
         ],
         compiler_params=pltpu.CompilerParams(vmem_limit_bytes=VMEM_MOST),

time: 310 us -> 309 us (level)
  the two profiles are of different devices: /device:TPU:30 before, /device:TPU:4 now
where the time goes in v6:
time: 309 us
  waiting for transfers between devices  160 us (52%)
  starting transfers between devices  61.7 us (20%)
  blocking collectives  45.4 us (15%)
  Pallas kernels  27.6 us (9%)
  local copies, waits for them, and re-layouts  7.02 us (2%)
  other arithmetic  3.8 us (1%)
    all_to_all x3, waiting for transfers between devices, exchange(): return lax.all_to_all(x, axis, 0, 0, tiled=True)  122 us
    ppermute x7, waiting for transfers between devices, far(): lax.ppermute(x, 'seq', [(i, (i + 2 * chips) % N_SEQ) for i in range(N_SEQ)])  37.1 us
    ppermute x7, starting transfers between devices, far(): lax.ppermute(x, 'seq', [(i, (i + 2 * chips) % N_SEQ) for i in range(N_SEQ)])  36.2 us
    all_to_all x3, starting transfers between devices, exchange(): return lax.all_to_all(x, axis, 0, 0, tiled=True)  23.6 us
    all_gather x1, blocking collectives, with_rows(): norm = jnp.sum(lax.all_gather(squares, 'head'), axis=0)  23.6 us
    all_gather x1, blocking collectives, with_rows(): spread = jnp.sum(lax.all_gather(spread, 'head'), axis=0)  21.9 us
    pallas_call x1, Pallas kernels, attention(): pl.pallas_call(functools.partial(attention_kernel, rows), in_specs=[vmem]...  9.46 us
    pallas_call x1, Pallas kernels, pack(): pl.pallas_call(functools.partial(pack_kernel, rows), grid=(PACK_STEPS,),...  8.88 us
  transfers between devices with their start and end apart: 11, of which 7 were waited for; matrix products, arithmetic and copies ran while one was open for 2% of the time, Pallas kernels for 0%

profile of v6, /device:TPU:4, one launch (start us, length us, event | category | flops | bytes accessed | tf_op | source)
XLA Modules:
  0.0 308.8 jit_solution(6047798809849865845)
XLA Ops:
  2.3 15.5 %all-to-all-start.4 = ((f32[32,1,256]{2,1,0:T(1,128)}), f32[32,1,256]{2,1,0:T(1,128)S(1)}, u32[]{:S(2)}, u32[]{:S(2)}) async-start(f32[32,1,256]{2,1,0:T(1,128)} %broadcast_in_dim.144), calls=%async_computation.4 | async-start | bytes 65536 | tf_op jit(solution)/shard_map/all_to_all | solution.py:309
  21.5 9.4 %all-to-all-done.4 = f32[32,1,256]{2,1,0:T(1,128)S(1)} async-done(((f32[32,1,256]{2,1,0:T(1,128)}), f32[32,1,256]{2,1,0:T(1,128)S(1)}, u32[]{:S(2)}, u32[]{:S(2)}) %all-to-all-start.4) | async-done | bytes 32800 | tf_op jit(solution)/shard_map/all_to_all | solution.py:309
  30.8 2.7 plan.1
  34.2 274.5 %conditional.1 = (bf16[2048,128]{1,0:T(8,128)(2,1)}, bf16[2048,128]{1,0:T(8,128)(2,1)}, bf16[2048,128]{1,0:T(8,128)(2,1)}, bf16[2048,128]{1,0:T(8,128)(2,1)}, f32[256,128]{1,0:T(8,128)}) conditional(s32[]{:T(128)} %bitcast.42, (f32[40,256]{1,0:T(8,128)S(1)}, s32[]{:T(128)}, f32[32,256]{1,0:T(8,128)S(1)}, s32[2048,1]{0,1:T(1,128)S(1)}, ...), branch_computations={%region_4.12_spmd, %region_12.20_spmd} | conditional | flops 39561232 | bytes 37014824 | solution.py:389
  34.4 8.9 %pack.3 = (bf16[2304,512]{1,0:T(8,128)(2,1)}, s32[1,2048]{1,0:T(1,128)}) custom-call(s32[1,1]{1,0:T(1,128)} %bitcast.20.seq_ref, f32[40,256]{1,0:T(8,128)S(1)} %get-tuple-element.60.plan_ref, s32[1,2048]{1,0:T(1,128)S(1)} %bitcast.122, s32[1,2048]{1,0:T(1,128)S(1)} %bitcast.124, bf16[2048,128]{1,0:T(8,128)(2,1)S(1)} %get-tuple-element.111.q_ref, ...), custom_call_target="tpu_custom_call" | custom-call | tf_op jit(solution)/shard_map/cond/branch_1_fun/pack/pallas_call | solution.py:93
  43.3 4.1 %all-to-all-start.2 = ((bf16[32,72,512]{2,1,0:T(8,128)(2,1)}), bf16[32,72,512]{2,1,0:T(8,128)(2,1)S(1)}, u32[]{:S(2)}, u32[]{:S(2)}) async-start(bf16[32,72,512]{2,1,0:T(8,128)(2,1)} %bitcast.114), calls=%async_computation.2 | async-start | bytes 4718592 | tf_op jit(solution)/shard_map/cond/branch_1_fun/all_to_all | solution.py:309
  48.6 111.5 %all-to-all-done.2 = bf16[32,72,512]{2,1,0:T(8,128)(2,1)S(1)} async-done(((bf16[32,72,512]{2,1,0:T(8,128)(2,1)}), bf16[32,72,512]{2,1,0:T(8,128)(2,1)S(1)}, u32[]{:S(2)}, u32[]{:S(2)}) %all-to-all-start.2) | async-done | bytes 2359328 | tf_op jit(solution)/shard_map/cond/branch_1_fun/all_to_all | solution.py:309
  160.1 9.5 %attention.3 = bf16[2304,512]{1,0:T(8,128)(2,1)S(1)} custom-call(s32[8,384]{1,0:T(8,128)S(1)} %reshape.528.place_ref, bf16[2304,512]{1,0:T(8,128)(2,1)S(1)} %bitcast.110), custom_call_target="tpu_custom_call" | custom-call | tf_op jit(solution)/shard_map/cond/branch_1_fun/attention/pallas_call | solution.py:226
  171.1 4.1 %all-to-all-start.3 = ((bf16[32,72,512]{2,1,0:T(8,128)(2,1)}), bf16[32,72,512]{2,1,0:T(8,128)(2,1)S(1)}, u32[]{:S(2)}, u32[]{:S(2)}) async-start(bf16[32,72,512]{2,1,0:T(8,128)(2,1)} %bitcast.112), calls=%async_computation.3 | async-start | bytes 4718592 | tf_op jit(solution)/shard_map/cond/branch_1_fun/all_to_all | solution.py:309
  176.0 23.6 %all-gather.3 = f32[16,1,2304]{2,1,0:T(1,128)S(1)} all-gather(f32[1,1,2304]{2,1,0:T(1,128)S(1)} %reshape.561), channel_id=1, replica_groups=mesh['seq'=32,'head'=16] {'head'}, dimensions={0}, use_global_device_ids=true | all-gather | bytes 156672 | tf_op jit(solution)/shard_map/cond/branch_1_fun/all_gather | solution.py:369
  200.9 21.9 %all-gather.1 = f32[128,128]{1,0:T(8,128)S(1)} all-gather(f32[8,128]{1,0:T(8,128)S(1)} %broadcast_in_dim.142), channel_id=3, replica_groups=mesh['seq'=32,'head'=16] {'head'}, dimensions={0}, use_global_device_ids=true | all-gather | bytes 69632 | tf_op jit(solution)/shard_map/cond/branch_1_fun/all_gather | solution.py:378
  222.7 1.9 collective-permute-start.8
  225.8 3.6 %collective-permute-start.9 = (f32[2,8,128]{2,1,0:T(8,128)S(1)}, f32[2,8,128]{2,1,0:T(8,128)S(1)}, u32[]{:S(2)}, u32[]{:S(2)}) collective-permute-start(f32[2,8,128]{2,1,0:T(8,128)S(1)} %pad_maximum_fusion.1), channel_id=1, source_target_pairs={{0,32},{16,48},{32,64},{48,80},{64,96},{80,112},{96,128},{112,144}... | collective-permute-start | bytes 24584 | tf_op jit(solution)/shard_map/cond/branch_1_fun/ppermute | solution.py:326
  229.4 4.3 %collective-permute-start.10 = (f32[2,8,128]{2,1,0:T(8,128)S(1)}, f32[2,8,128]{2,1,0:T(8,128)S(1)}, u32[]{:S(2)}, u32[]{:S(2)}) collective-permute-start(f32[2,8,128]{2,1,0:T(8,128)S(1)} %pad_maximum_fusion.1), channel_id=1, source_target_pairs={{0,64},{16,80},{32,96},{48,112},{64,128},{80,144},{96,160},{112,17... | collective-permute-start | bytes 24584 | tf_op jit(solution)/shard_map/cond/branch_1_fun/ppermute | solution.py:326
  233.7 6.4 %collective-permute-start.11 = (f32[2,8,128]{2,1,0:T(8,128)S(1)}, f32[2,8,128]{2,1,0:T(8,128)S(1)}, u32[]{:S(2)}, u32[]{:S(2)}) collective-permute-start(f32[2,8,128]{2,1,0:T(8,128)S(1)} %pad_maximum_fusion.1), channel_id=1, source_target_pairs={{0,96},{16,112},{32,128},{48,144},{64,160},{80,176},{96,192},{112,... | collective-permute-start | bytes 24584 | tf_op jit(solution)/shard_map/cond/branch_1_fun/ppermute | solution.py:326
  240.1 5.5 %collective-permute-start.12 = (f32[2,8,128]{2,1,0:T(8,128)S(1)}, f32[2,8,128]{2,1,0:T(8,128)S(1)}, u32[]{:S(2)}, u32[]{:S(2)}) collective-permute-start(f32[2,8,128]{2,1,0:T(8,128)S(1)} %pad_maximum_fusion.1), channel_id=1, source_target_pairs={{0,128},{16,144},{32,160},{48,176},{64,192},{80,208},{96,224},{112... | collective-permute-start | bytes 24584 | tf_op jit(solution)/shard_map/cond/branch_1_fun/ppermute | solution.py:326
  245.7 2.5 collective-permute-start.13
  248.2 27.8 %collective-permute-done.9 = f32[2,8,128]{2,1,0:T(8,128)S(1)} collective-permute-done((f32[2,8,128]{2,1,0:T(8,128)S(1)}, f32[2,8,128]{2,1,0:T(8,128)S(1)}, u32[]{:S(2)}, u32[]{:S(2)}) %collective-permute-start.9) | collective-permute-done | bytes 8224 | tf_op jit(solution)/shard_map/cond/branch_1_fun/ppermute | solution.py:326
  276.0 6.8 %collective-permute-done.10 = f32[2,8,128]{2,1,0:T(8,128)S(1)} collective-permute-done((f32[2,8,128]{2,1,0:T(8,128)S(1)}, f32[2,8,128]{2,1,0:T(8,128)S(1)}, u32[]{:S(2)}, u32[]{:S(2)}) %collective-permute-start.10) | collective-permute-done | bytes 8224 | tf_op jit(solution)/shard_map/cond/branch_1_fun/ppermute | solution.py:326
  282.9 1.6 all-to-all-done.3
  284.5 6.6 %unpack.3 = (bf16[2048,128]{1,0:T(8,128)(2,1)}, bf16[2048,128]{1,0:T(8,128)(2,1)}, bf16[2048,128]{1,0:T(8,128)(2,1)}, bf16[2048,128]{1,0:T(8,128)(2,1)}) custom-call(s32[2048,1]{1,0:T(8,128)S(1)} %copy.52.place_ref, bf16[2304,512]{1,0:T(8,128)(2,1)S(1)} %bitcast.111), custom_call_target="tpu_custom_call" | custom-call | tf_op jit(solution)/shard_map/cond/branch_1_fun/unpack/pallas_call | solution.py:129
  291.1 5.8 %collective-permute-start.14 = (f32[12,8,128]{2,1,0:T(8,128)S(1)}, f32[12,8,128]{2,1,0:T(8,128)S(1)}, u32[]{:S(2)}, u32[]{:S(2)}) collective-permute-start(f32[12,8,128]{2,1,0:T(8,128)S(1)} %constant_dynamic-update-slice_fusion.7), channel_id=1, source_target_pairs={{0,192},{16,208},{32,224},{48,240},{64,256},{80,272},{96,288},{112... | collective-permute-start | bytes 147464 | tf_op jit(solution)/shard_map/cond/branch_1_fun/ppermute | solution.py:326
  296.9 8.0 %collective-permute-start.15 = (f32[12,8,128]{2,1,0:T(8,128)S(1)}, f32[12,8,128]{2,1,0:T(8,128)S(1)}, u32[]{:S(2)}, u32[]{:S(2)}) collective-permute-start(f32[12,8,128]{2,1,0:T(8,128)S(1)} %constant_dynamic-update-slice_fusion.7), channel_id=1, source_target_pairs={{0,384},{16,400},{32,416},{48,432},{64,448},{80,464},{96,480},{112... | collective-permute-start | bytes 147464 | tf_op jit(solution)/shard_map/cond/branch_1_fun/ppermute | solution.py:326
  304.9 2.5 collective-permute-done.15
  (71 shorter events, 12.5 us)
Async XLA Ops:
  2.3 28.5 %all-to-all-start.4 = ((f32[32,1,256]{2,1,0:T(1,128)}), f32[32,1,256]{2,1,0:T(1,128)S(1)}, u32[]{:S(2)}, u32[]{:S(2)}) async-start(f32[32,1,256]{2,1,0:T(1,128)} %broadcast_in_dim.144), calls=%async_computation.4 | async-start | bytes 65536 | tf_op jit(solution)/shard_map/all_to_all | solution.py:309
  19.3 1.3 copy-start.5
  20.5 13.7 %copy-start.3 = (bf16[2048,128]{1,0:T(8,128)(2,1)S(1)}, bf16[2048,128]{1,0:T(8,128)(2,1)}, u32[]{:S(2)}) copy-start(bf16[2048,128]{1,0:T(8,128)(2,1)} %param.7) | copy-start | bytes 1572868
  20.5 13.7 %copy-start.4 = (bf16[2048,128]{1,0:T(8,128)(2,1)S(1)}, bf16[2048,128]{1,0:T(8,128)(2,1)}, u32[]{:S(2)}) copy-start(bf16[2048,128]{1,0:T(8,128)(2,1)} %param.8) | copy-start | bytes 1572868
  43.3 116.8 %all-to-all-start.2 = ((bf16[32,72,512]{2,1,0:T(8,128)(2,1)}), bf16[32,72,512]{2,1,0:T(8,128)(2,1)S(1)}, u32[]{:S(2)}, u32[]{:S(2)}) async-start(bf16[32,72,512]{2,1,0:T(8,128)(2,1)} %bitcast.114), calls=%async_computation.2 | async-start | bytes 4718592 | tf_op jit(solution)/shard_map/cond/branch_1_fun/all_to_all | solution.py:309
  169.6 1.4 copy-start.1
  171.1 113.4 %all-to-all-start.3 = ((bf16[32,72,512]{2,1,0:T(8,128)(2,1)}), bf16[32,72,512]{2,1,0:T(8,128)(2,1)S(1)}, u32[]{:S(2)}, u32[]{:S(2)}) async-start(bf16[32,72,512]{2,1,0:T(8,128)(2,1)} %bitcast.112), calls=%async_computation.3 | async-start | bytes 4718592 | tf_op jit(solution)/shard_map/cond/branch_1_fun/all_to_all | solution.py:309
  175.2 49.5 %copy-start.7 = (s32[1,2048]{1,0:T(1,128)S(1)}, s32[1,2048]{1,0:T(1,128)}, u32[]{:S(2)}) copy-start(s32[1,2048]{1,0:T(1,128)} %get-tuple-element.69) | copy-start | bytes 24580 | tf_op jit(solution)/shard_map/cond
  222.7 3.1 collective-permute-start.8
  225.8 50.2 %collective-permute-start.9 = (f32[2,8,128]{2,1,0:T(8,128)S(1)}, f32[2,8,128]{2,1,0:T(8,128)S(1)}, u32[]{:S(2)}, u32[]{:S(2)}) collective-permute-start(f32[2,8,128]{2,1,0:T(8,128)S(1)} %pad_maximum_fusion.1), channel_id=1, source_target_pairs={{0,32},{16,48},{32,64},{48,80},{64,96},{80,112},{96,128},{112,144}... | collective-permute-start | bytes 24584 | tf_op jit(solution)/shard_map/cond/branch_1_fun/ppermute | solution.py:326
  229.4 53.4 %collective-permute-start.10 = (f32[2,8,128]{2,1,0:T(8,128)S(1)}, f32[2,8,128]{2,1,0:T(8,128)S(1)}, u32[]{:S(2)}, u32[]{:S(2)}) collective-permute-start(f32[2,8,128]{2,1,0:T(8,128)S(1)} %pad_maximum_fusion.1), channel_id=1, source_target_pairs={{0,64},{16,80},{32,96},{48,112},{64,128},{80,144},{96,160},{112,17... | collective-permute-start | bytes 24584 | tf_op jit(solution)/shard_map/cond/branch_1_fun/ppermute | solution.py:326
  233.7 49.1 %collective-permute-start.11 = (f32[2,8,128]{2,1,0:T(8,128)S(1)}, f32[2,8,128]{2,1,0:T(8,128)S(1)}, u32[]{:S(2)}, u32[]{:S(2)}) collective-permute-start(f32[2,8,128]{2,1,0:T(8,128)S(1)} %pad_maximum_fusion.1), channel_id=1, source_target_pairs={{0,96},{16,112},{32,128},{48,144},{64,160},{80,176},{96,192},{112,... | collective-permute-start | bytes 24584 | tf_op jit(solution)/shard_map/cond/branch_1_fun/ppermute | solution.py:326
  240.1 42.7 %collective-permute-start.12 = (f32[2,8,128]{2,1,0:T(8,128)S(1)}, f32[2,8,128]{2,1,0:T(8,128)S(1)}, u32[]{:S(2)}, u32[]{:S(2)}) collective-permute-start(f32[2,8,128]{2,1,0:T(8,128)S(1)} %pad_maximum_fusion.1), channel_id=1, source_target_pairs={{0,128},{16,144},{32,160},{48,176},{64,192},{80,208},{96,224},{112... | collective-permute-start | bytes 24584 | tf_op jit(solution)/shard_map/cond/branch_1_fun/ppermute | solution.py:326
  245.7 37.2 %collective-permute-start.13 = (f32[2,8,128]{2,1,0:T(8,128)S(1)}, f32[2,8,128]{2,1,0:T(8,128)S(1)}, u32[]{:S(2)}, u32[]{:S(2)}) collective-permute-start(f32[2,8,128]{2,1,0:T(8,128)S(1)} %pad_maximum_fusion.1), channel_id=1, source_target_pairs={{0,160},{16,176},{32,192},{48,208},{64,224},{80,240},{96,256},{112... | collective-permute-start | bytes 24584 | tf_op jit(solution)/shard_map/cond/branch_1_fun/ppermute | solution.py:326
  291.1 13.8 %collective-permute-start.14 = (f32[12,8,128]{2,1,0:T(8,128)S(1)}, f32[12,8,128]{2,1,0:T(8,128)S(1)}, u32[]{:S(2)}, u32[]{:S(2)}) collective-permute-start(f32[12,8,128]{2,1,0:T(8,128)S(1)} %constant_dynamic-update-slice_fusion.7), channel_id=1, source_target_pairs={{0,192},{16,208},{32,224},{48,240},{64,256},{80,272},{96,288},{112... | collective-permute-start | bytes 147464 | tf_op jit(solution)/shard_map/cond/branch_1_fun/ppermute | solution.py:326
  296.9 10.5 %collective-permute-start.15 = (f32[12,8,128]{2,1,0:T(8,128)S(1)}, f32[12,8,128]{2,1,0:T(8,128)S(1)}, u32[]{:S(2)}, u32[]{:S(2)}) collective-permute-start(f32[12,8,128]{2,1,0:T(8,128)S(1)} %constant_dynamic-update-slice_fusion.7), channel_id=1, source_target_pairs={{0,384},{16,400},{32,416},{48,432},{64,448},{80,464},{96,480},{112... | collective-permute-start | bytes 147464 | tf_op jit(solution)/shard_map/cond/branch_1_fun/ppermute | solution.py:326

commit v7 on v6

--- a/solution.py
+++ b/solution.py
@@ -21,7 +21,7 @@
 ROWS_FULL = OWN * CAPC
 PACK_STEPS = 4
 EPSILON = 1e-06
-NEAR = 6
+NEAR = 8
 HIDDEN = 1e30
 LOG2E = 1.4426950408889634
 SIDE_BY_SIDE = 4

time: 309 us -> 326 us (1.055)
  the two profiles are of different devices: /device:TPU:4 before, /device:TPU:10 now
where the time goes in v7:
time: 326 us; the launch traced here: 325 us
  waiting for transfers between devices  170 us (52%)
  starting transfers between devices  69.1 us (21%)
  blocking collectives  44.7 us (14%)
  Pallas kernels  27.6 us (8%)
  local copies, waits for them, and re-layouts  7.03 us (2%)
  other arithmetic  3.8 us (1%)
    all_to_all x3, waiting for transfers between devices, exchange(): return lax.all_to_all(x, axis, 0, 0, tiled=True)  121 us
    ppermute x8, waiting for transfers between devices, far(): lax.ppermute(x, 'seq', [(i, (i + 2 * chips) % N_SEQ) for i in range(N_SEQ)])  48.2 us
    ppermute x8, starting transfers between devices, far(): lax.ppermute(x, 'seq', [(i, (i + 2 * chips) % N_SEQ) for i in range(N_SEQ)])  43.6 us
    all_to_all x3, starting transfers between devices, exchange(): return lax.all_to_all(x, axis, 0, 0, tiled=True)  23.6 us
    all_gather x1, blocking collectives, with_rows(): spread = jnp.sum(lax.all_gather(spread, 'head'), axis=0)  22.4 us
    all_gather x1, blocking collectives, with_rows(): norm = jnp.sum(lax.all_gather(squares, 'head'), axis=0)  22.3 us
    pallas_call x1, Pallas kernels, attention(): pl.pallas_call(functools.partial(attention_kernel, rows), in_specs=[vmem]...  9.46 us
    pallas_call x1, Pallas kernels, pack(): pl.pallas_call(functools.partial(pack_kernel, rows), grid=(PACK_STEPS,),...  8.88 us
  transfers between devices with their start and end apart: 12, of which 6 were waited for; matrix products, arithmetic and copies ran while one was open for 2% of the time, Pallas kernels for 0%

profile of v7, /device:TPU:10, one launch (start us, length us, event | category | flops | bytes accessed | tf_op | source)
XLA Modules:
  0.0 325.1 jit_solution(7205871810473114298)
XLA Ops:
  2.3 15.5 %all-to-all-start.4 = ((f32[32,1,256]{2,1,0:T(1,128)}), f32[32,1,256]{2,1,0:T(1,128)S(1)}, u32[]{:S(2)}, u32[]{:S(2)}) async-start(f32[32,1,256]{2,1,0:T(1,128)} %broadcast_in_dim.144), calls=%async_computation.4 | async-start | bytes 65536 | tf_op jit(solution)/shard_map/all_to_all | solution.py:309
  21.5 9.4 %all-to-all-done.4 = f32[32,1,256]{2,1,0:T(1,128)S(1)} async-done(((f32[32,1,256]{2,1,0:T(1,128)}), f32[32,1,256]{2,1,0:T(1,128)S(1)}, u32[]{:S(2)}, u32[]{:S(2)}) %all-to-all-start.4) | async-done | bytes 32800 | tf_op jit(solution)/shard_map/all_to_all | solution.py:309
  30.8 2.7 plan.1
  34.2 290.8 %conditional.1 = (bf16[2048,128]{1,0:T(8,128)(2,1)}, bf16[2048,128]{1,0:T(8,128)(2,1)}, bf16[2048,128]{1,0:T(8,128)(2,1)}, bf16[2048,128]{1,0:T(8,128)(2,1)}, f32[256,128]{1,0:T(8,128)}) conditional(s32[]{:T(128)} %bitcast.42, (f32[40,256]{1,0:T(8,128)S(1)}, s32[]{:T(128)}, f32[32,256]{1,0:T(8,128)S(1)}, s32[2048,1]{0,1:T(1,128)S(1)}, ...), branch_computations={%region_4.12_spmd, %region_12.20_spmd} | conditional | flops 39520272 | bytes 36949328 | solution.py:389
  34.4 8.9 %pack.3 = (bf16[2304,512]{1,0:T(8,128)(2,1)}, s32[1,2048]{1,0:T(1,128)}) custom-call(s32[1,1]{1,0:T(1,128)} %bitcast.20.seq_ref, f32[40,256]{1,0:T(8,128)S(1)} %get-tuple-element.60.plan_ref, s32[1,2048]{1,0:T(1,128)S(1)} %bitcast.122, s32[1,2048]{1,0:T(1,128)S(1)} %bitcast.124, bf16[2048,128]{1,0:T(8,128)(2,1)S(1)} %get-tuple-element.111.q_ref, ...), custom_call_target="tpu_custom_call" | custom-call | tf_op jit(solution)/shard_map/cond/branch_1_fun/pack/pallas_call | solution.py:93
  43.3 4.1 %all-to-all-start.2 = ((bf16[32,72,512]{2,1,0:T(8,128)(2,1)}), bf16[32,72,512]{2,1,0:T(8,128)(2,1)S(1)}, u32[]{:S(2)}, u32[]{:S(2)}) async-start(bf16[32,72,512]{2,1,0:T(8,128)(2,1)} %bitcast.114), calls=%async_computation.2 | async-start | bytes 4718592 | tf_op jit(solution)/shard_map/cond/branch_1_fun/all_to_all | solution.py:309
  48.6 111.5 %all-to-all-done.2 = bf16[32,72,512]{2,1,0:T(8,128)(2,1)S(1)} async-done(((bf16[32,72,512]{2,1,0:T(8,128)(2,1)}), bf16[32,72,512]{2,1,0:T(8,128)(2,1)S(1)}, u32[]{:S(2)}, u32[]{:S(2)}) %all-to-all-start.2) | async-done | bytes 2359328 | tf_op jit(solution)/shard_map/cond/branch_1_fun/all_to_all | solution.py:309
  160.1 9.5 %attention.3 = bf16[2304,512]{1,0:T(8,128)(2,1)S(1)} custom-call(s32[8,384]{1,0:T(8,128)S(1)} %reshape.528.place_ref, bf16[2304,512]{1,0:T(8,128)(2,1)S(1)} %bitcast.110), custom_call_target="tpu_custom_call" | custom-call | tf_op jit(solution)/shard_map/cond/branch_1_fun/attention/pallas_call | solution.py:226
  171.1 4.1 %all-to-all-start.3 = ((bf16[32,72,512]{2,1,0:T(8,128)(2,1)}), bf16[32,72,512]{2,1,0:T(8,128)(2,1)S(1)}, u32[]{:S(2)}, u32[]{:S(2)}) async-start(bf16[32,72,512]{2,1,0:T(8,128)(2,1)} %bitcast.112), calls=%async_computation.3 | async-start | bytes 4718592 | tf_op jit(solution)/shard_map/cond/branch_1_fun/all_to_all | solution.py:309
  176.0 22.3 %all-gather.3 = f32[16,1,2304]{2,1,0:T(1,128)S(1)} all-gather(f32[1,1,2304]{2,1,0:T(1,128)S(1)} %reshape.561), channel_id=1, replica_groups=mesh['seq'=32,'head'=16] {'head'}, dimensions={0}, use_global_device_ids=true | all-gather | bytes 156672 | tf_op jit(solution)/shard_map/cond/branch_1_fun/all_gather | solution.py:369
  199.6 22.4 %all-gather.1 = f32[128,128]{1,0:T(8,128)S(1)} all-gather(f32[8,128]{1,0:T(8,128)S(1)} %broadcast_in_dim.142), channel_id=3, replica_groups=mesh['seq'=32,'head'=16] {'head'}, dimensions={0}, use_global_device_ids=true | all-gather | bytes 69632 | tf_op jit(solution)/shard_map/cond/branch_1_fun/all_gather | solution.py:378
  222.0 1.9 collective-permute-start.9
  225.1 3.6 %collective-permute-start.10 = (f32[2,8,128]{2,1,0:T(8,128)S(1)}, f32[2,8,128]{2,1,0:T(8,128)S(1)}, u32[]{:S(2)}, u32[]{:S(2)}) collective-permute-start(f32[2,8,128]{2,1,0:T(8,128)S(1)} %pad_maximum_fusion.1), channel_id=1, source_target_pairs={{0,32},{16,48},{32,64},{48,80},{64,96},{80,112},{96,128},{112,144}... | collective-permute-start | bytes 24584 | tf_op jit(solution)/shard_map/cond/branch_1_fun/ppermute | solution.py:326
  228.7 4.3 %collective-permute-start.11 = (f32[2,8,128]{2,1,0:T(8,128)S(1)}, f32[2,8,128]{2,1,0:T(8,128)S(1)}, u32[]{:S(2)}, u32[]{:S(2)}) collective-permute-start(f32[2,8,128]{2,1,0:T(8,128)S(1)} %pad_maximum_fusion.1), channel_id=1, source_target_pairs={{0,64},{16,80},{32,96},{48,112},{64,128},{80,144},{96,160},{112,17... | collective-permute-start | bytes 24584 | tf_op jit(solution)/shard_map/cond/branch_1_fun/ppermute | solution.py:326
  233.0 6.4 %collective-permute-start.12 = (f32[2,8,128]{2,1,0:T(8,128)S(1)}, f32[2,8,128]{2,1,0:T(8,128)S(1)}, u32[]{:S(2)}, u32[]{:S(2)}) collective-permute-start(f32[2,8,128]{2,1,0:T(8,128)S(1)} %pad_maximum_fusion.1), channel_id=1, source_target_pairs={{0,96},{16,112},{32,128},{48,144},{64,160},{80,176},{96,192},{112,... | collective-permute-start | bytes 24584 | tf_op jit(solution)/shard_map/cond/branch_1_fun/ppermute | solution.py:326
  239.4 5.5 %collective-permute-start.13 = (f32[2,8,128]{2,1,0:T(8,128)S(1)}, f32[2,8,128]{2,1,0:T(8,128)S(1)}, u32[]{:S(2)}, u32[]{:S(2)}) collective-permute-start(f32[2,8,128]{2,1,0:T(8,128)S(1)} %pad_maximum_fusion.1), channel_id=1, source_target_pairs={{0,128},{16,144},{32,160},{48,176},{64,192},{80,208},{96,224},{112... | collective-permute-start | bytes 24584 | tf_op jit(solution)/shard_map/cond/branch_1_fun/ppermute | solution.py:326
  245.0 2.5 collective-permute-start.14
  247.5 28.5 %collective-permute-done.10 = f32[2,8,128]{2,1,0:T(8,128)S(1)} collective-permute-done((f32[2,8,128]{2,1,0:T(8,128)S(1)}, f32[2,8,128]{2,1,0:T(8,128)S(1)}, u32[]{:S(2)}, u32[]{:S(2)}) %collective-permute-start.10) | collective-permute-done | bytes 8224 | tf_op jit(solution)/shard_map/cond/branch_1_fun/ppermute | solution.py:326
  276.0 10.8 %collective-permute-start.15 = (f32[2,8,128]{2,1,0:T(8,128)S(1)}, f32[2,8,128]{2,1,0:T(8,128)S(1)}, u32[]{:S(2)}, u32[]{:S(2)}) collective-permute-start(f32[2,8,128]{2,1,0:T(8,128)S(1)} %pad_maximum_fusion.1), channel_id=1, source_target_pairs={{0,192},{16,208},{32,224},{48,240},{64,256},{80,272},{96,288},{112... | collective-permute-start | bytes 24584 | tf_op jit(solution)/shard_map/cond/branch_1_fun/ppermute | solution.py:326
  286.8 5.1 %collective-permute-start.16 = (f32[2,8,128]{2,1,0:T(8,128)S(1)}, f32[2,8,128]{2,1,0:T(8,128)S(1)}, u32[]{:S(2)}, u32[]{:S(2)}) collective-permute-start(f32[2,8,128]{2,1,0:T(8,128)S(1)} %pad_maximum_fusion.1), channel_id=1, source_target_pairs={{0,224},{16,240},{32,256},{48,272},{64,288},{80,304},{96,320},{112... | collective-permute-start | bytes 24584 | tf_op jit(solution)/shard_map/cond/branch_1_fun/ppermute | solution.py:326
  292.0 8.3 %collective-permute-done.16 = f32[2,8,128]{2,1,0:T(8,128)S(1)} collective-permute-done((f32[2,8,128]{2,1,0:T(8,128)S(1)}, f32[2,8,128]{2,1,0:T(8,128)S(1)}, u32[]{:S(2)}, u32[]{:S(2)}) %collective-permute-start.16) | collective-permute-done | bytes 8224 | tf_op jit(solution)/shard_map/cond/branch_1_fun/ppermute | solution.py:326
  300.3 6.6 %unpack.3 = (bf16[2048,128]{1,0:T(8,128)(2,1)}, bf16[2048,128]{1,0:T(8,128)(2,1)}, bf16[2048,128]{1,0:T(8,128)(2,1)}, bf16[2048,128]{1,0:T(8,128)(2,1)}) custom-call(s32[2048,1]{1,0:T(8,128)S(1)} %copy.52.place_ref, bf16[2304,512]{1,0:T(8,128)(2,1)S(1)} %bitcast.111), custom_call_target="tpu_custom_call" | custom-call | tf_op jit(solution)/shard_map/cond/branch_1_fun/unpack/pallas_call | solution.py:129
  306.9 5.4 %collective-permute-start.17 = (f32[16,8,128]{2,1,0:T(8,128)S(1)}, f32[16,8,128]{2,1,0:T(8,128)S(1)}, u32[]{:S(2)}, u32[]{:S(2)}) collective-permute-start(f32[16,8,128]{2,1,0:T(8,128)S(1)} %constant_dynamic-update-slice_fusion.9), channel_id=1, source_target_pairs={{0,256},{16,272},{32,288},{48,304},{64,320},{80,336},{96,352},{112... | collective-permute-start | bytes 196616 | tf_op jit(solution)/shard_map/cond/branch_1_fun/ppermute | solution.py:326
  312.3 11.4 %collective-permute-done.17 = f32[16,8,128]{2,1,0:T(8,128)S(1)} collective-permute-done((f32[16,8,128]{2,1,0:T(8,128)S(1)}, f32[16,8,128]{2,1,0:T(8,128)S(1)}, u32[]{:S(2)}, u32[]{:S(2)}) %collective-permute-start.17) | collective-permute-done | bytes 65568 | tf_op jit(solution)/shard_map/cond/branch_1_fun/ppermute | solution.py:326
  (75 shorter events, 12.5 us)
Async XLA Ops:
  2.3 28.5 %all-to-all-start.4 = ((f32[32,1,256]{2,1,0:T(1,128)}), f32[32,1,256]{2,1,0:T(1,128)S(1)}, u32[]{:S(2)}, u32[]{:S(2)}) async-start(f32[32,1,256]{2,1,0:T(1,128)} %broadcast_in_dim.144), calls=%async_computation.4 | async-start | bytes 65536 | tf_op jit(solution)/shard_map/all_to_all | solution.py:309
  19.3 1.3 copy-start.5
  20.5 13.7 %copy-start.3 = (bf16[2048,128]{1,0:T(8,128)(2,1)S(1)}, bf16[2048,128]{1,0:T(8,128)(2,1)}, u32[]{:S(2)}) copy-start(bf16[2048,128]{1,0:T(8,128)(2,1)} %param.7) | copy-start | bytes 1572868
  20.5 13.7 %copy-start.4 = (bf16[2048,128]{1,0:T(8,128)(2,1)S(1)}, bf16[2048,128]{1,0:T(8,128)(2,1)}, u32[]{:S(2)}) copy-start(bf16[2048,128]{1,0:T(8,128)(2,1)} %param.8) | copy-start | bytes 1572868
  43.3 116.8 %all-to-all-start.2 = ((bf16[32,72,512]{2,1,0:T(8,128)(2,1)}), bf16[32,72,512]{2,1,0:T(8,128)(2,1)S(1)}, u32[]{:S(2)}, u32[]{:S(2)}) async-start(bf16[32,72,512]{2,1,0:T(8,128)(2,1)} %bitcast.114), calls=%async_computation.2 | async-start | bytes 4718592 | tf_op jit(solution)/shard_map/cond/branch_1_fun/all_to_all | solution.py:309
  169.6 1.4 copy-start.1
  171.1 129.2 %all-to-all-start.3 = ((bf16[32,72,512]{2,1,0:T(8,128)(2,1)}), bf16[32,72,512]{2,1,0:T(8,128)(2,1)S(1)}, u32[]{:S(2)}, u32[]{:S(2)}) async-start(bf16[32,72,512]{2,1,0:T(8,128)(2,1)} %bitcast.112), calls=%async_computation.3 | async-start | bytes 4718592 | tf_op jit(solution)/shard_map/cond/branch_1_fun/all_to_all | solution.py:309
  175.2 48.8 %copy-start.7 = (s32[1,2048]{1,0:T(1,128)S(1)}, s32[1,2048]{1,0:T(1,128)}, u32[]{:S(2)}) copy-start(s32[1,2048]{1,0:T(1,128)} %get-tuple-element.69) | copy-start | bytes 24580 | tf_op jit(solution)/shard_map/cond
  222.0 3.1 collective-permute-start.9
  225.1 50.9 %collective-permute-start.10 = (f32[2,8,128]{2,1,0:T(8,128)S(1)}, f32[2,8,128]{2,1,0:T(8,128)S(1)}, u32[]{:S(2)}, u32[]{:S(2)}) collective-permute-start(f32[2,8,128]{2,1,0:T(8,128)S(1)} %pad_maximum_fusion.1), channel_id=1, source_target_pairs={{0,32},{16,48},{32,64},{48,80},{64,96},{80,112},{96,128},{112,144}... | collective-permute-start | bytes 24584 | tf_op jit(solution)/shard_map/cond/branch_1_fun/ppermute | solution.py:326
  228.7 58.1 %collective-permute-start.11 = (f32[2,8,128]{2,1,0:T(8,128)S(1)}, f32[2,8,128]{2,1,0:T(8,128)S(1)}, u32[]{:S(2)}, u32[]{:S(2)}) collective-permute-start(f32[2,8,128]{2,1,0:T(8,128)S(1)} %pad_maximum_fusion.1), channel_id=1, source_target_pairs={{0,64},{16,80},{32,96},{48,112},{64,128},{80,144},{96,160},{112,17... | collective-permute-start | bytes 24584 | tf_op jit(solution)/shard_map/cond/branch_1_fun/ppermute | solution.py:326
  233.0 58.9 %collective-permute-start.12 = (f32[2,8,128]{2,1,0:T(8,128)S(1)}, f32[2,8,128]{2,1,0:T(8,128)S(1)}, u32[]{:S(2)}, u32[]{:S(2)}) collective-permute-start(f32[2,8,128]{2,1,0:T(8,128)S(1)} %pad_maximum_fusion.1), channel_id=1, source_target_pairs={{0,96},{16,112},{32,128},{48,144},{64,160},{80,176},{96,192},{112,... | collective-permute-start | bytes 24584 | tf_op jit(solution)/shard_map/cond/branch_1_fun/ppermute | solution.py:326
  239.4 52.5 %collective-permute-start.13 = (f32[2,8,128]{2,1,0:T(8,128)S(1)}, f32[2,8,128]{2,1,0:T(8,128)S(1)}, u32[]{:S(2)}, u32[]{:S(2)}) collective-permute-start(f32[2,8,128]{2,1,0:T(8,128)S(1)} %pad_maximum_fusion.1), channel_id=1, source_target_pairs={{0,128},{16,144},{32,160},{48,176},{64,192},{80,208},{96,224},{112... | collective-permute-start | bytes 24584 | tf_op jit(solution)/shard_map/cond/branch_1_fun/ppermute | solution.py:326
  245.0 47.0 %collective-permute-start.14 = (f32[2,8,128]{2,1,0:T(8,128)S(1)}, f32[2,8,128]{2,1,0:T(8,128)S(1)}, u32[]{:S(2)}, u32[]{:S(2)}) collective-permute-start(f32[2,8,128]{2,1,0:T(8,128)S(1)} %pad_maximum_fusion.1), channel_id=1, source_target_pairs={{0,160},{16,176},{32,192},{48,208},{64,224},{80,240},{96,256},{112... | collective-permute-start | bytes 24584 | tf_op jit(solution)/shard_map/cond/branch_1_fun/ppermute | solution.py:326
  276.0 16.0 %collective-permute-start.15 = (f32[2,8,128]{2,1,0:T(8,128)S(1)}, f32[2,8,128]{2,1,0:T(8,128)S(1)}, u32[]{:S(2)}, u32[]{:S(2)}) collective-permute-start(f32[2,8,128]{2,1,0:T(8,128)S(1)} %pad_maximum_fusion.1), channel_id=1, source_target_pairs={{0,192},{16,208},{32,224},{48,240},{64,256},{80,272},{96,288},{112... | collective-permute-start | bytes 24584 | tf_op jit(solution)/shard_map/cond/branch_1_fun/ppermute | solution.py:326
  286.8 13.5 %collective-permute-start.16 = (f32[2,8,128]{2,1,0:T(8,128)S(1)}, f32[2,8,128]{2,1,0:T(8,128)S(1)}, u32[]{:S(2)}, u32[]{:S(2)}) collective-permute-start(f32[2,8,128]{2,1,0:T(8,128)S(1)} %pad_maximum_fusion.1), channel_id=1, source_target_pairs={{0,224},{16,240},{32,256},{48,272},{64,288},{80,304},{96,320},{112... | collective-permute-start | bytes 24584 | tf_op jit(solution)/shard_map/cond/branch_1_fun/ppermute | solution.py:326
  306.9 16.8 %collective-permute-start.17 = (f32[16,8,128]{2,1,0:T(8,128)S(1)}, f32[16,8,128]{2,1,0:T(8,128)S(1)}, u32[]{:S(2)}, u32[]{:S(2)}) collective-permute-start(f32[16,8,128]{2,1,0:T(8,128)S(1)} %constant_dynamic-update-slice_fusion.9), channel_id=1, source_target_pairs={{0,256},{16,272},{32,288},{48,304},{64,320},{80,336},{96,352},{112... | collective-permute-start | bytes 196616 | tf_op jit(solution)/shard_map/cond/branch_1_fun/ppermute | solution.py:326
